TPU v7x, 256 devices: a whole 4x4x8 slice. The times are simulated.
256 devices in a mesh: grp: 4 (over x), seq: 16 (over z, core), dp: 4 (over y).
Axes of the slice: x: 4, y: 4, z: 8, core: 2. Of those that a mesh axis runs over, the one named last changes fastest.
Arguments:
- item_hidden: bfloat16 [32768, 2048], P(('grp', 'seq', 'dp')), may hold values from -6 to 6
- item_gain: float32 [2048], replicated, may hold values from 0.25 to 1.75
- slot_owner: int32 [32, 1024, 1], P(('grp', 'dp'), 'seq'), may hold values from 0 to 63; in each aligned block of 64 rows (0 to 63, 64 to 127, ..., all dimensions but the last counted through in order) at most 2 rows name the same one
- slot_row: int32 [32, 1024], P(('grp', 'dp'), 'seq'), may hold values from 0 to 127
- seq_count: int32 [32], P(('grp', 'dp')), may hold values from 1 to 1024, 20480 in all
- user_gain: float32 [2048], replicated, may hold values from 0.25 to 1.75
- query_key_value_weight: bfloat16 [3, 2048, 2048], P(None, None, 'seq'), as said below
- d_out: bfloat16 [32, 1024, 2048], P(('grp', 'dp'), None, 'seq'), may hold values from -6 to 6
Outputs:
- attn_out: bfloat16 [32, 1024, 2048], P(('grp', 'dp'), None, 'seq')
- d_hidden: bfloat16 [32768, 2048], P(('grp', 'seq', 'dp'))
- grad_qkv: float32 [3, 2048, 2048], P(None, None, 'seq')
- grad_user_gain: float32 [2048], replicated
- grad_item_gain: float32 [2048], replicated
Inputs may be any that keep to these rules, and one draw needn't show every extreme that they name: `slot_owner`: within each sequence, each aligned block of 64 positions names one owner at most 2 times; some block reaches it. `seq_count`: every sequence has one live slot or more, the live slots first. `query_key_value_weight`: projection weights of order fan-in to the minus one half.
All inputs are finite; a program needn't handle non-finite values. No bound on the sum of `seq_count` on one device may be relied on, other than what follows from the above.
Results may differ from a plain program's by a relative error of at most 0.025.
The roundings to bfloat16 on the way count: a program that leaves them out, or rounds other values in their place, can miss the bound.
Values may be sent and summed in bfloat16 or wider, within the bound.
A program may use at most 128 MiB of HBM per device.

v0:
```python
import math

import jax
import jax.numpy as jnp
from jax import lax
from jax.sharding import PartitionSpec as P

HD = 128


epsilon = 1e-05


def norm_rows(values, gain_row):
    factor = lax.rsqrt(jnp.mean(values * values, axis=-1, keepdims=True) + epsilon)
    return (values * factor * gain_row, factor)


def norm_back(values, factor, gain_row, incoming):
    weighted = gain_row * incoming
    return factor * weighted - values * factor * factor * factor * jnp.mean(
        weighted * values, axis=-1, keepdims=True
    )


def head_math(query, keys, values, upstream, live_count):
    length = query.shape[0]
    factor = 1.0 / math.sqrt(query.shape[-1])
    scores = jnp.einsum("qhd,khd->hqk", query, keys, preferred_element_type=jnp.float32) * factor
    places = jnp.arange(length, dtype=jnp.int32)
    allowed = (places[None, :] <= places[:, None]) & (places[None, :] < live_count)
    scores = jnp.where(allowed[None], scores, -1e30)
    highest = jnp.max(scores, axis=-1, keepdims=True)
    exponent = jnp.exp(scores - highest)
    weights_f = exponent / jnp.sum(exponent, axis=-1, keepdims=True)
    weights_b = weights_f.astype(jnp.bfloat16)
    result = jnp.einsum(
        "hqk,khd->qhd", weights_b, values, preferred_element_type=jnp.float32
    ).astype(jnp.bfloat16)
    d_weights = jnp.einsum("qhd,khd->hqk", upstream, values, preferred_element_type=jnp.float32)
    d_values = jnp.einsum(
        "hqk,qhd->khd", weights_b, upstream, preferred_element_type=jnp.float32
    ).astype(jnp.bfloat16)
    center = jnp.sum(weights_f * d_weights, axis=-1, keepdims=True)
    d_scores = (weights_f * (d_weights - center) * factor).astype(jnp.bfloat16)
    d_query = jnp.einsum("hqk,khd->qhd", d_scores, keys, preferred_element_type=jnp.float32).astype(
        jnp.bfloat16
    )
    d_keys = jnp.einsum("hqk,qhd->khd", d_scores, query, preferred_element_type=jnp.float32).astype(
        jnp.bfloat16
    )
    return (result, d_query, d_keys, d_values)


def local(
    item_hidden,
    item_gain,
    slot_owner,
    slot_row,
    seq_count,
    user_gain,
    query_key_value_weight,
    d_out,
):
    seq_devices = lax.axis_size("seq")
    dp_devices = lax.axis_size("dp")
    owners = seq_devices * dp_devices
    seq_here, local_len, unused_dim = slot_owner.shape
    rows_here = seq_here * local_len
    items_here, model_width = item_hidden.shape
    per_block = max(2, 2 * local_len // owners)
    capacity = seq_here * per_block
    slots_all = owners * capacity
    hidden_f = item_hidden.astype(jnp.float32)
    item_normed, item_factor = norm_rows(hidden_f, item_gain)
    embedded = item_normed.astype(jnp.bfloat16)
    owner_flat = slot_owner.reshape(rows_here)
    row_flat = slot_row.reshape(rows_here)
    member = (owner_flat[:, None] == jnp.arange(owners, dtype=jnp.int32)[None, :]).astype(jnp.int32)
    earlier = jnp.cumsum(member, axis=0) - member
    ranked = jnp.sum(earlier * member, axis=1)
    position = owner_flat * capacity + ranked
    requests = jnp.full((slots_all,), -1, jnp.int32).at[position].set(row_flat)
    placing = position[:, None] == jnp.arange(slots_all, dtype=jnp.int32)[None, :]
    asked_rows = lax.all_to_all(
        requests.reshape(owners, capacity), ("seq", "dp"), split_axis=0, concat_axis=0, tiled=True
    )
    picking_rows = (asked_rows[..., None] == jnp.arange(items_here, dtype=jnp.int32)).astype(
        jnp.bfloat16
    )
    arrived = lax.all_to_all(
        jnp.einsum(
            "...j,jd->...d", picking_rows, embedded, preferred_element_type=jnp.float32
        ).astype(jnp.bfloat16),
        ("seq", "dp"),
        split_axis=0,
        concat_axis=0,
        tiled=True,
    )
    received = asked_rows
    arrived = arrived.reshape(slots_all, model_width)
    received = received.reshape(slots_all)
    inputs_f = jnp.dot(placing.astype(jnp.bfloat16), arrived, preferred_element_type=jnp.float32)
    inputs_f = inputs_f.reshape(seq_here, local_len, model_width)
    user_normed, user_factor = norm_rows(inputs_f, user_gain)
    normed = user_normed.astype(jnp.bfloat16)
    collected_rows = lax.all_gather(normed, "seq", axis=1, tiled=True)
    full_len = collected_rows.shape[1]
    local_width = query_key_value_weight.shape[2]
    head_count = local_width // HD
    projected = jnp.einsum(
        "fqv,zvk->fqzk", collected_rows, query_key_value_weight, preferred_element_type=jnp.float32
    ).astype(jnp.bfloat16)
    projected = projected.reshape(seq_here, full_len, 3, head_count, HD)
    upstream = d_out.reshape(seq_here, full_len, head_count, HD)

    def per_seq(packed):
        projected_seq, live_count, upstream_seq = packed
        return head_math(
            projected_seq[:, 0], projected_seq[:, 1], projected_seq[:, 2], upstream_seq, live_count
        )

    result, d_query, d_keys, d_values = lax.map(per_seq, (projected, seq_count, upstream))
    attn_out = result.reshape(seq_here, full_len, local_width)
    projection_gradient = jnp.stack([d_query, d_keys, d_values], axis=2).reshape(
        seq_here, full_len, 3, local_width
    )
    local_gradient = jnp.einsum(
        "nyg,nyji->jgi", collected_rows, projection_gradient, preferred_element_type=jnp.float32
    )
    grad_qkv = lax.psum(local_gradient.astype(jnp.bfloat16), ("grp", "dp")).astype(jnp.float32)
    partial_totals_sum = jnp.einsum(
        "zqni,noi->zqo",
        projection_gradient,
        query_key_value_weight,
        preferred_element_type=jnp.float32,
    )
    d_normed = lax.psum_scatter(
        partial_totals_sum.astype(jnp.bfloat16), "seq", scatter_dimension=1, tiled=True
    ).astype(jnp.float32)
    user_terms = jnp.sum(d_normed * inputs_f * user_factor, axis=(0, 1))
    d_inputs = norm_back(inputs_f, user_factor, user_gain, d_normed).reshape(rows_here, model_width)
    outgoing = jnp.einsum(
        "rs,rd->sd", placing.astype(jnp.float32), d_inputs, precision=lax.Precision.HIGHEST
    )
    returned = lax.all_to_all(
        outgoing.reshape(owners, capacity, model_width).astype(jnp.bfloat16),
        ("seq", "dp"),
        split_axis=0,
        concat_axis=0,
        tiled=True,
    ).astype(jnp.float32)
    returned = returned.reshape(slots_all, model_width)
    picking = (received[:, None] == jnp.arange(items_here, dtype=jnp.int32)[None, :]).astype(
        jnp.float32
    )
    d_embedded = jnp.einsum("rj,rd->jd", picking, returned, precision=lax.Precision.HIGHEST)
    item_terms = jnp.sum(d_embedded * hidden_f * item_factor, axis=0)
    d_hidden = norm_back(hidden_f, item_factor, item_gain, d_embedded).astype(jnp.bfloat16)
    grad_user_gain, grad_item_gain = lax.psum((user_terms, item_terms), ("grp", "seq", "dp"))
    return (attn_out, d_hidden, grad_qkv, grad_user_gain, grad_item_gain)


def solution(mesh):
    in_specs = (
        P(("grp", "seq", "dp"), None),
        P(),
        P(("grp", "dp"), "seq", None),
        P(("grp", "dp"), "seq"),
        P(("grp", "dp")),
        P(),
        P(None, None, "seq"),
        P(("grp", "dp"), None, "seq"),
    )
    out_specs = (
        P(("grp", "dp"), None, "seq"),
        P(("grp", "seq", "dp"), None),
        P(None, None, "seq"),
        P(),
        P(),
    )
    return jax.shard_map(local, mesh=mesh, in_specs=in_specs, out_specs=out_specs, check_vma=False)
```

profile of v0, /device:TPU:1, one launch (start us, length us, event | category | flops | bytes accessed | tf_op | source)
XLA Modules:
  0.0 452.4 jit_solution(8370438507299777263)
XLA Ops:
  7.2 0.9 reshape.234
  8.6 1.3 fusion.75
  10.5 1.0 scatter_custom_fusion
  12.2 13.2 %all-to-all-start = ((s32[64,1,4]{2,1,0:T(1,128)}), s32[64,1,4]{2,1,0:T(1,128)S(1)}, u32[]{:S(2)}, u32[]{:S(2)}) async-start(s32[64,1,4]{2,1,0:T(1,128)} %bitcast.22), calls=%async_computation | async-start | bytes 65536 | tf_op jit(solution)/shard_map/all_to_all | solution.py:85
  25.4 1.2 fusion.50
  26.6 7.8 %all-to-all-done = s32[64,1,4]{2,1,0:T(1,128)S(1)} async-done(((s32[64,1,4]{2,1,0:T(1,128)}), s32[64,1,4]{2,1,0:T(1,128)S(1)}, u32[]{:S(2)}, u32[]{:S(2)}) %all-to-all-start) | async-done | bytes 1056 | tf_op jit(solution)/shard_map/all_to_all | solution.py:85
  34.6 1.6 convolution_convert_fusion.4
  36.1 1.8 copy.33
  37.9 5.8 %all-to-all-start.1 = ((bf16[64,4,2048]{2,1,0:T(4,128)(2,1)}), bf16[64,4,2048]{2,1,0:T(4,128)(2,1)}, u32[]{:S(2)}, u32[]{:S(2)}) async-start(bf16[64,4,2048]{2,1,0:T(4,128)(2,1)} %copy.33), calls=%async_computation.1 | async-start | bytes 2097152 | tf_op jit(solution)/shard_map/all_to_all | solution.py:91
  43.9 27.6 %all-to-all-done.1 = bf16[64,4,2048]{2,1,0:T(4,128)(2,1)} async-done(((bf16[64,4,2048]{2,1,0:T(4,128)(2,1)}), bf16[64,4,2048]{2,1,0:T(4,128)(2,1)}, u32[]{:S(2)}, u32[]{:S(2)}) %all-to-all-start.1) | async-done | bytes 1048608 | tf_op jit(solution)/shard_map/all_to_all | solution.py:91
  71.5 1.3 reshape.239
  73.3 1.0 copy-done.1
  74.2 0.9 multiply_convert_fusion.1
  75.3 53.5 %all-gather.2.cloned.1.call-done = bf16[2,1024,2048]{2,1,0:T(8,128)(2,1)} async-done(((bf16[2,64,2048]{2,1,0:T(8,128)(2,1)}), bf16[2,1024,2048]{2,1,0:T(8,128)(2,1)}) %all-gather.2.cloned.1.call-update) | async-done | bytes 8388624 | tf_op jit(solution)/shard_map/all_gather | solution.py:107
  128.9 9.0 %fusion.32 = bf16[2,1024,3,1,128]{4,1,3,2,0:T(8,128)(2,1)} fusion(bf16[3,2048,128]{2,1,0:T(8,128)(2,1)S(1)} %copy-done, bf16[2,1024,2048]{2,1,0:T(8,128)(2,1)} %all-gather.2.cloned.1.call-done), kind=kOutput, calls=%fused_computation.54 | convolution fusion | flops 3222011904 | bytes 11534336 | tf_op jit(solution)/shard_map/fqv,zvk->fqzk/dot_general | solution.py:111
  137.9 25.1 %while.16 = (s32[]{:T(128)}, bf16[2,1024,1,128]{3,1,0,2:T(8,128)(2,1)}, bf16[2,1024,1,128]{3,1,0,2:T(8,128)(2,1)}, bf16[2,1024,1,128]{3,1,0,2:T(8,128)(2,1)}, bf...) while((s32[]{:T(128)}, ...), condition=%wide.region_9.10_spmd, body=%wide.region_5.9_spmd.sunk | while | flops 1637349376 | bytes 52985992 | solution.py:123
  139.1 1.2 dynamic-slice_bitcast_fusion.2
  140.2 0.8 fusion.98
  141.0 1.9 fusion.99
  143.0 1.3 multiply_reduce_fusion.3
  144.3 1.1 multiply_convert_fusion.3
  145.4 0.8 fusion.103
  147.2 0.9 fusion.102
  148.8 0.8 constant_dynamic-update-slice_fusion.7
  149.6 0.8 constant_dynamic-update-slice_fusion.6
  151.6 1.2 dynamic-slice_bitcast_fusion.2
  153.5 1.9 fusion.99
  155.5 1.3 multiply_reduce_fusion.3
  156.8 1.1 multiply_convert_fusion.3
  157.9 0.8 fusion.103
  159.7 0.9 fusion.102
  161.3 0.9 constant_dynamic-update-slice_fusion.7
  162.2 0.8 constant_dynamic-update-slice_fusion.6
  163.0 8.2 %bitcast_convert_fusion = bf16[2,1024,2048]{2,1,0:T(8,128)(2,1)} fusion(bf16[3,2048,128]{2,1,0:T(8,128)(2,1)S(1)} %copy-done, bf16[2,1024,1,1,128]{4,1,2,0,3:T(8,128)(2,1)} %bitcast.161, bf16[2,1024,1,1,128]{4,1,2,0,3:T(8,128)(2,1)} %bitcast.163, bf16[2,1024,1,1,128]{4,1,2,0,3:T(8,128)(2,1)} %bitcast.165), kind=kOutput, calls=%fused_computation.37 | convolution fusion | flops 3226992640 | bytes 11534336 | tf_op jit(solution)/shard_map/zqni,noi->zqo/dot_general | solution.py:132
  171.2 65.9 %reduce-scatter.2.cloned.1.call-done = bf16[2,64,2048]{2,1,0:T(8,128)(2,1)} async-done(((bf16[2,1024,2048]{2,1,0:T(8,128)(2,1)}), bf16[2,64,2048]{2,1,0:T(8,128)(2,1)}) %reduce-scatter.2.cloned.1.call-update) | async-done | bytes 524304 | tf_op jit(solution)/shard_map/reduce_scatter | solution.py:138
  237.1 1.4 fusion.49
  238.5 1.4 fusion.46
  239.9 1.0 convolution_convert_fusion.5
  240.9 1.9 copy.40
  242.8 11.1 %all-to-all-start.2 = ((bf16[64,4,2048]{2,1,0:T(4,128)(2,1)}), bf16[64,4,2048]{2,1,0:T(4,128)(2,1)S(1)}, u32[]{:S(2)}, u32[]{:S(2)}) async-start(bf16[64,4,2048]{2,1,0:T(4,128)(2,1)} %copy.40), calls=%async_computation.3 | async-start | bytes 2097152 | tf_op jit(solution)/shard_map/all_to_all | solution.py:146
  254.0 8.4 %fusion.24 = bf16[3,2048,128]{1,2,0:T(8,128)(2,1)} fusion(bf16[2,1024,2048]{2,1,0:T(8,128)(2,1)} %all-gather.2.cloned.1.call-done, bf16[2,1024,1,1,128]{4,1,2,0,3:T(8,128)(2,1)S(1)} %bitcast.162, bf16[2,1024,1,1,128]{4,1,2,0,3:T(8,128)(2,1)} %bitcast.164, bf16[2,1024,1,1,128]{4,1,2,0,3:T(8,128)(2,1)} %bitcast.166), kind=kOutput, calls=%fused_computation.43 | convolution fusion | flops 3223584768 | bytes 11534336 | tf_op jit(solution)/shard_map/nyg,nyji->jgi/dot_general | solution.py:128
  262.4 0.8 reduce.17
  263.3 98.2 %all-reduce.3.cloned.1.call-done = bf16[3,2048,128]{1,2,0:T(8,128)(2,1)} async-done(((bf16[3,2048,128]{1,2,0:T(8,128)(2,1)}), bf16[3,2048,128]{1,2,0:T(8,128)(2,1)}) %all-reduce.3.cloned.1.call-update) | async-done | bytes 1572880 | tf_op jit(solution)/shard_map/psum | solution.py:131
  361.5 3.1 copy.42
  364.6 1.1 reshape.229
  365.7 1.8 fusion.53
  367.6 77.1 %all-reduce = (f32[2048]{0:T(1024)}, f32[2048]{0:T(1024)}) all-reduce(f32[2048]{0:T(1024)S(1)} %get-tuple-element.95, f32[2048]{0:T(1024)S(1)} %get-tuple-element.93), channel_id=1, replica_groups=mesh['grp'=4,'seq'=16,'dp'=4] {'grp','seq','dp'}, use_global_device_ids=true, to_apply=%region_15.16 | all-reduce | flops 4096 | bytes 32768 | tf_op jit(solution)/shard_map/psum | solution.py:160
  444.7 1.1 fusion.45
  (64 shorter events, 9.0 us)
Async XLA Ops:
  7.2 121.7 %copy-start = (bf16[3,2048,128]{2,1,0:T(8,128)(2,1)S(1)}, bf16[3,2048,128]{2,1,0:T(8,128)(2,1)}, u32[]{:S(2)}) copy-start(bf16[3,2048,128]{2,1,0:T(8,128)(2,1)} %param.16) | copy-start | bytes 4718596
  12.2 22.2 %all-to-all-start = ((s32[64,1,4]{2,1,0:T(1,128)}), s32[64,1,4]{2,1,0:T(1,128)S(1)}, u32[]{:S(2)}, u32[]{:S(2)}) async-start(s32[64,1,4]{2,1,0:T(1,128)} %bitcast.22), calls=%async_computation | async-start | bytes 65536 | tf_op jit(solution)/shard_map/all_to_all | solution.py:85
  36.1 38.1 %copy-start.5 = (f32[2048]{0:T(1024)S(1)}, f32[2048]{0:T(1024)}, u32[]{:S(2)}) copy-start(f32[2048]{0:T(1024)} %param.15) | copy-start | bytes 24580
  37.9 33.5 %all-to-all-start.1 = ((bf16[64,4,2048]{2,1,0:T(4,128)(2,1)}), bf16[64,4,2048]{2,1,0:T(4,128)(2,1)}, u32[]{:S(2)}, u32[]{:S(2)}) async-start(bf16[64,4,2048]{2,1,0:T(4,128)(2,1)} %copy.33), calls=%async_computation.1 | async-start | bytes 2097152 | tf_op jit(solution)/shard_map/all_to_all | solution.py:91
  43.8 85.1 %all-gather.2.cloned.1.call-start = ((), (), s32[]{:S(2)}) async-start(), calls=%async_computation.4 | async-start | bytes 8912896 | tf_op jit(solution)/shard_map/all_gather | solution.py:107
  73.2 1.0 copy-start.1
  75.2 161.9 %reduce-scatter.2.cloned.1.call-start = ((), (), s32[]{:S(2)}) async-start(), calls=%async_computation.5 | async-start | bytes 8912896 | tf_op jit(solution)/shard_map/reduce_scatter | solution.py:138
  75.3 62.6 %copy-start.4 = (bf16[2,1024,128]{2,1,0:T(8,128)(2,1)S(1)}, bf16[2,1024,128]{2,1,0:T(8,128)(2,1)}, u32[]{:S(2)}) copy-start(bf16[2,1024,128]{2,1,0:T(8,128)(2,1)} %param.17) | copy-start | bytes 1572868
  75.3 62.6 %copy-start.8 = (s32[2]{0:T(128)S(1)}, s32[2]{0:T(128)}, u32[]{:S(2)}) copy-start(s32[2]{0:T(128)} %param.14) | copy-start | bytes 28
  171.2 66.0 %copy-start.2 = (f32[2,64,2048]{2,1,0:T(8,128)S(1)}, f32[2,64,2048]{2,1,0:T(8,128)}, u32[]{:S(2)}) copy-start(f32[2,64,2048]{2,1,0:T(8,128)} %copy-done.1) | copy-start | bytes 3145732
  239.9 14.1 %copy-start.7 = (bf16[2,1024,1,128]{3,1,0,2:T(8,128)(2,1)S(1)}, bf16[2,1024,1,128]{3,1,0,2:T(8,128)(2,1)}, u32[]{:S(2)}) copy-start(bf16[2,1024,1,128]{3,1,0,2:T(8,128)(2,1)} %get-tuple-element.53) | copy-start | bytes 1572868
  242.8 121.8 %all-to-all-start.2 = ((bf16[64,4,2048]{2,1,0:T(4,128)(2,1)}), bf16[64,4,2048]{2,1,0:T(4,128)(2,1)S(1)}, u32[]{:S(2)}, u32[]{:S(2)}) async-start(bf16[64,4,2048]{2,1,0:T(4,128)(2,1)} %copy.40), calls=%async_computation.3 | async-start | bytes 2097152 | tf_op jit(solution)/shard_map/all_to_all | solution.py:146
  253.9 107.6 %all-reduce.3.cloned.1.call-start = ((), (), s32[]{:S(2)}) async-start(), calls=%async_computation.6 | async-start | bytes 3145728 | tf_op jit(solution)/shard_map/psum | solution.py:131
  262.3 103.4 %copy-start.3 = (bf16[128,2048]{1,0:T(8,128)(2,1)S(1)}, bf16[128,2048]{1,0:T(8,128)(2,1)}, u32[]{:S(2)}) copy-start(bf16[128,2048]{1,0:T(8,128)(2,1)} %param.10) | copy-start | bytes 1572868
  262.3 103.4 %copy-start.6 = (f32[2048]{0:T(1024)S(1)}, f32[2048]{0:T(1024)}, u32[]{:S(2)}) copy-start(f32[2048]{0:T(1024)} %param.11) | copy-start | bytes 24580
Sparse Core Ops, SparseCore 0:
  75.3 53.4 all-gather.1
  171.3 65.7 reduce-scatter.1
  262.5 98.9 all-reduce.2
where the time goes:
time: 453 us; the launch traced here: 452 us
  waiting for transfers between devices  253 us (56%)
  blocking collectives  77.1 us (17%)
  matrix products  39.8 us (9%)
  starting transfers between devices  30.2 us (7%)
  local copies, waits for them, and re-layouts  21.9 us (5%)
  other arithmetic  15.9 us (4%)
  between operations  14 us (3%)
    psum x1, waiting for transfers between devices, local(): lax.psum(local_gradient.astype(jnp.bfloat16), ('grp', 'dp'))  98.2 us
    psum x1, blocking collectives, local(): lax.psum((user_terms, item_terms), ('grp', 'seq', 'dp'))  77.1 us
    reduce_scatter x1, waiting for transfers between devices, local(): lax.psum_scatter(partial_totals_sum.astype(jnp.bfloat16), 'seq', scatter_...  65.9 us
    all_gather x1, waiting for transfers between devices, local(): collected_rows = lax.all_gather(normed, 'seq', axis=1, tiled=True)  53.5 us
    all_to_all x1, waiting for transfers between devices, local(): lax.all_to_all(jnp.einsum('...j,jd->...d', picking_rows, embedded, prefer...  27.6 us
    all_to_all x1, starting transfers between devices, local(): lax.all_to_all(requests.reshape(owners, capacity), ('seq', 'dp'), split_a...  13.2 us
    all_to_all x1, starting transfers between devices, local(): lax.all_to_all(outgoing.reshape(owners, capacity, model_width).astype(jnp...  11.1 us
  transfers between devices with their start and end apart: 6, of which 5 were waited for; matrix products, arithmetic and copies ran while one was open for 3% of the time, Pallas kernels for 0%

commit v1 on v0

v1 whole, which is shorter than its diff:
```python
import functools
import math

import jax
import jax.numpy as jnp
from jax import lax
from jax.experimental import pallas as pl
from jax.experimental.pallas import tpu as pltpu
from jax.sharding import PartitionSpec as P

HD = 128
LANES = 128
Q = 4
EPS = 1e-05
MESH = pl.DeviceIdType.MESH
F32, BF16 = jnp.float32, jnp.bfloat16
VMEM_LIMIT = 60 * 2**20


def iota(shape, dim):
    return lax.broadcasted_iota(jnp.int32, shape, dim).astype(F32)


def onehot(mask):
    return jnp.where(mask, 1.0, 0.0).astype(BF16)


def column(row):
    return jnp.broadcast_to(row, (LANES, LANES)).T


def plane_peer(index, nd):
    return {"seq": index // nd, "dp": lax.rem(index, nd)}


def greet(barrier, device):
    pl.semaphore_signal(barrier, inc=1, device_id=device, device_id_type=MESH)


def remote(src, dst, send, recv, device):
    return pltpu.make_async_remote_copy(
        src_ref=src, dst_ref=dst, send_sem=send, recv_sem=recv, device_id=device, device_id_type=MESH
    )


def slots(ids_ref, cap):
    owner_row = ids_ref[0:1, :].astype(F32)
    owner = jnp.broadcast_to(owner_row, (LANES, LANES))
    same = jnp.where(owner == owner.T, 1.0, 0.0)
    before = iota((LANES, LANES), 0) < iota((LANES, LANES), 1)
    rank_row = jnp.sum(jnp.where(before, same, 0.0), axis=0, keepdims=True)
    return owner_row, rank_row, (owner_row * cap + rank_row) * Q


def fetch_kernel(
    ns, nd, cap, ids_ref, hidden_ref, igain_ref, ugain_ref,
    normed_ref, inputs_ref, ufactor_ref, val_ref,
    req, reqr, table, out, arr, id_send, id_recv, row_send, row_recv,
):
    owners, msg = ns * nd, cap * Q
    per = LANES // msg
    groups = owners // per
    width = hidden_ref.shape[1]
    part = width // Q
    items = hidden_ref.shape[0]
    me = lax.axis_index("seq") * nd + lax.axis_index("dp")
    barrier = pltpu.get_barrier_semaphore()

    @pl.loop(1, owners)
    def _(i):
        greet(barrier, plane_peer(lax.rem(me + i, owners), nd))

    owner_row, rank_row, base_row = slots(ids_ref, cap)
    lane = lax.broadcasted_iota(jnp.int32, (LANES, LANES), 1)
    slot_in = ((lane % msg) // Q).astype(F32)
    piece = (lane % Q).astype(F32)
    row_col = column(ids_ref[1:2, :].astype(F32) + 1.0)
    rank_col = column(rank_row)
    wanted = jnp.where(rank_col == slot_in, row_col, 0.0).astype(BF16)
    names = onehot(iota((owners, LANES), 0) == owner_row)
    asked = jnp.dot(names, wanted, preferred_element_type=F32)
    asked = jnp.where(asked > 0.5, asked - 1.0 + piece[0:1, :] * items, -1.0).astype(jnp.int32)
    for o in range(owners):
        req[o] = asked[o : o + 1, :]

    pl.semaphore_wait(barrier, owners - 1)

    @pl.loop(1, owners)
    def _(i):
        peer = lax.rem(me + i, owners)
        remote(req.at[peer], reqr.at[me], id_send, id_recv, plane_peer(peer, nd)).start()

    reqr[me] = req[me]
    hidden = hidden_ref[...].astype(F32)
    factor = lax.rsqrt(jnp.mean(hidden * hidden, axis=-1, keepdims=True) + EPS)
    for q in range(Q):
        cols = slice(q * part, (q + 1) * part)
        piece_f = hidden_ref[:, cols].astype(F32)
        table[q * items : (q + 1) * items, :] = (piece_f * factor * igain_ref[:, cols]).astype(BF16)
    remote(
        req.at[pl.ds(0, owners - 1)], reqr.at[pl.ds(0, owners - 1)], id_send, id_recv, plane_peer(me, nd)
    ).wait()

    lane_group = lax.broadcasted_iota(jnp.int32, (1, LANES), 1) // msg
    my_group = me // per
    for step in range(groups):
        turn = (step + 1) // 2 if step % 2 else groups - step // 2
        g = lax.rem(my_group + turn, groups)
        val = jnp.zeros((1, LANES), jnp.int32)
        for k in range(per):
            val = jnp.where(lane_group == k, reqr[g * per + k], val)
        val_ref[g] = val
        col = column(val.astype(F32))
        pick = jnp.concatenate([onehot(col == iota((LANES, LANES), 1) + q * items) for q in range(Q)], axis=1)
        picked = jnp.dot(pick, table[...], preferred_element_type=F32).astype(BF16)
        out[pl.ds(g * per, per)] = picked.reshape(per, msg, part)
        for k in range(per):
            peer = g * per + k

            @pl.when(peer != me)
            def _():
                remote(out.at[peer], arr.at[me], row_send, row_recv, plane_peer(peer, nd)).start()

    arr[me] = out[me]
    base_col = column(base_row)
    remote(
        out.at[pl.ds(0, owners - 1)], arr.at[pl.ds(0, owners - 1)], row_send, row_recv, plane_peer(me, nd)
    ).wait()
    arrived = arr[...].reshape(owners * msg, part)
    total = jnp.zeros((LANES, 1), F32)
    for q in range(Q):
        place = jnp.concatenate(
            [onehot(iota((LANES, LANES), 1) + t * LANES == base_col + q) for t in range(groups)], axis=1
        )
        rows = jnp.dot(place, arrived, preferred_element_type=F32)
        inputs_ref[:, q * part : (q + 1) * part] = rows.astype(BF16)
        total += jnp.sum(rows * rows, axis=-1, keepdims=True)
    ufactor = lax.rsqrt(total / width + EPS)
    ufactor_ref[...] = ufactor
    normed_ref[...] = (inputs_ref[...].astype(F32) * ufactor * ugain_ref[...]).astype(BF16)


def fetch(ns, nd, cap, ids, hidden, igain, ugain):
    items, width = hidden.shape
    owners, msg = ns * nd, cap * Q
    vmem = pl.BlockSpec(memory_space=pltpu.VMEM)
    return pl.pallas_call(
        functools.partial(fetch_kernel, ns, nd, cap),
        out_shape=(
            jax.ShapeDtypeStruct((LANES, width), BF16),
            jax.ShapeDtypeStruct((LANES, width), BF16),
            jax.ShapeDtypeStruct((LANES, 1), F32),
            jax.ShapeDtypeStruct((owners * msg // LANES, 1, LANES), jnp.int32),
        ),
        in_specs=[vmem] * 4,
        out_specs=[vmem] * 4,
        scratch_shapes=[
            pltpu.VMEM((owners, 1, LANES), jnp.int32),
            pltpu.VMEM((owners, 1, LANES), jnp.int32),
            pltpu.VMEM((Q * items, width // Q), BF16),
            pltpu.VMEM((owners, msg, width // Q), BF16),
            pltpu.VMEM((owners, msg, width // Q), BF16),
        ]
        + [pltpu.SemaphoreType.DMA] * 4,
        compiler_params=pltpu.CompilerParams(
            collective_id=0, has_side_effects=True, vmem_limit_bytes=VMEM_LIMIT
        ),
        name="fetch",
    )(ids, hidden, igain, ugain)


def layer_kernel(
    ns, count_ref, normed_ref, inputs_ref, ufactor_ref, ugain_ref, weight_ref, dout_ref,
    attn_ref, grad_ref, dinputs_ref, uterms_ref,
    gat, prj, dpr, dpt, wgt, part, mix, ring, dk_acc, dv_acc,
    ag_send, ag_recv, sb_send, sb_recv, mx_send, mx_recv, rs_send, rs_recv,
):
    seqs, _, local_len, width = gat.shape
    length = ns * local_len
    nz = ns // 2
    half = nz // 2
    hops = 2 * half - 1
    hl = local_len // 2
    per = 4
    tile = per * local_len
    tiles = ns // per
    me = lax.axis_index("seq")
    z, core = me // 2, lax.rem(me, 2)
    sib = {"seq": me + 1 - 2 * core}
    sib_index = me + 1 - 2 * core
    ahead = ({"seq": lax.rem(me + 2, ns)}, {"seq": lax.rem(me + ns - 2, ns)})
    scale = 1.0 / math.sqrt(HD)

    barrier = pltpu.get_barrier_semaphore()
    for device in (*ahead, sib):
        greet(barrier, device)
    for f in range(seqs):
        gat[f, me] = normed_ref[f * local_len : (f + 1) * local_len, :]
    pl.semaphore_wait(barrier, 3)

    def ag_place(f, d, e, origin):
        far = e // 2
        h = d if e == hops - 1 else e % 2
        block = lax.rem(origin + (ns - 2 * far if d == 0 else 2 * far), ns)
        return gat.at[f, block, pl.ds(h * hl, hl)]

    def ag_copy(f, d, e):
        ref = ag_place(f, d, e, me)
        return remote(ref, ref, ag_send.at[f, d, e], ag_recv.at[f, d, e], ahead[d])

    def ag_arrival(f, d, e, at):
        behind = lax.rem(at + (ns - 2 if d == 0 else 2), ns)
        return ag_place(f, d, e, behind)

    def ag_wait(f, d, e):
        ref = ag_arrival(f, d, e, me)
        remote(ref, ref, ag_send.at[f, d, e], ag_recv.at[f, d, e], ahead[d]).wait_recv()

    def sb_copy(f, n):
        ref = gat.at[f, me] if n == 0 else ag_arrival(f, (n - 1) % 2, (n - 1) // 2, me)
        return remote(ref, ref, sb_send.at[f, n], sb_recv.at[f, n], sib)

    def sb_wait(f, n):
        ref = gat.at[f, sib_index] if n == 0 else ag_arrival(f, (n - 1) % 2, (n - 1) // 2, sib_index)
        remote(ref, ref, sb_send.at[f, n], sb_recv.at[f, n], sib).wait_recv()

    def ag_begin(f):
        for e in range(min(2, hops)):
            for d in range(2):
                ag_copy(f, d, e).start()
        sb_copy(f, 0).start()

    def ag_event(f, d, e):
        ag_wait(f, d, e)
        if e + 2 < hops - 1:
            ag_copy(f, d, e + 2).start()
        elif e + 2 == hops - 1 + d:
            ag_copy(f, d, hops - 1).start()
        sb_copy(f, 1 + 2 * e + d).start()

    def ag_events(f):
        return [functools.partial(ag_event, f, d, e) for e in range(hops) for d in range(2)]

    def ag_end(f):
        for n in range(1 + 2 * hops):
            sb_wait(f, n)

    order = [(half, None)] + [(t, h) for t in range(half - 1, 0, -1) for h in range(2)]

    def rs_what(d, i):
        t, h = order[i]
        return t, d if h is None else h

    def chip(d, t):
        return lax.rem(z + (t if d == 0 else nz - t), nz)

    def rs_copy(f, d, i):
        t, h = rs_what(d, i)
        return remote(
            mix.at[f, chip(d, t), pl.ds(h * hl, hl)], ring.at[f, d, i], rs_send.at[f, d, i], rs_recv.at[f, d, i], ahead[d]
        )

    def mx_copy(f, k):
        return remote(part.at[f, 2 * k + 1 - core], mix.at[f, k], mx_send.at[f, k], mx_recv.at[f, k], sib)

    def own_sum(f, k):
        mix[f, k] = (mix[f, k].astype(F32) + part[f, 2 * k + core].astype(F32)).astype(BF16)

    def rs_begin(f):
        for k in range(nz):
            mx_copy(f, k).wait_recv()

    def rs_own(f, t):
        own_sum(f, chip(0, t))
        if 0 < t < half:
            own_sum(f, chip(1, t))
        if t == half:
            for d in range(2):
                rs_copy(f, d, 0).start()
        elif t > 0:
            for d in range(2):
                for i in range(len(order)):
                    if rs_what(d, i)[0] == t and rs_source(d, i) is None:
                        rs_copy(f, d, i).start()

    def rs_source(d, i):
        t, h = rs_what(d, i)
        for j in range(len(order)):
            if rs_what(d, j) == (t + 1, h):
                return j
        return None

    def rs_event(f, d, j):
        rs_copy(f, d, j).wait_recv()
        t, h = rs_what(d, j)
        if t == 1:
            return
        for i in range(len(order)):
            if rs_what(d, i) == (t - 1, h):
                rows = pl.ds(h * hl, hl)
                k = chip(d, t - 1)
                mix[f, k, rows] = (mix[f, k, rows].astype(F32) + ring[f, d, j].astype(F32)).astype(BF16)
                rs_copy(f, d, i).start()

    def rs_events(f):
        out = [functools.partial(rs_begin, f)]
        out += [functools.partial(rs_own, f, t) for t in range(half, -1, -1)]
        return out + [functools.partial(rs_event, f, d, j) for j in range(len(order)) for d in range(2)]

    def rs_end(f):
        total = mix[f, z].astype(F32)
        for h in range(2):
            rows = slice(h * hl, (h + 1) * hl)
            got = total[rows]
            for d in range(2):
                for i in range(len(order)):
                    if rs_what(d, i) == (1, h):
                        got = got + ring[f, d, i].astype(F32)
            at = slice(f * local_len + h * hl, f * local_len + (h + 1) * hl)
            values = inputs_ref[at, :].astype(F32)
            factor = ufactor_ref[at, :]
            term = jnp.sum(got * values * factor, axis=0, keepdims=True)
            if f == 0 and h == 0:
                uterms_ref[...] = term
            else:
                uterms_ref[...] += term
            weighted = ugain_ref[...] * got
            center = jnp.mean(weighted * values, axis=-1, keepdims=True)
            dinputs_ref[at, :] = (factor * weighted - values * (factor * factor * factor * center)).astype(BF16)

    def project(f, i):
        rows = gat[f, i * per : (i + 1) * per].reshape(tile, width)
        prj[f, i * tile : (i + 1) * tile, :] = jnp.dot(rows, wgt[...], preferred_element_type=F32).astype(BF16)

    def attend(f, i):
        keys_n = (i + 1) * tile
        at = slice(i * tile, (i + 1) * tile)
        query = prj[f, at, 0:HD]
        keys = prj[f, 0:keys_n, HD : 2 * HD]
        values = prj[f, 0:keys_n, 2 * HD : 3 * HD]
        upstream = dout_ref[f, at, :]
        over = (((1,), (1,)), ((), ()))
        down = (((0,), (0,)), ((), ()))
        scores = lax.dot_general(query, keys, over, preferred_element_type=F32) * scale
        p = lax.broadcasted_iota(jnp.int32, (tile, keys_n), 0) + i * tile
        k = lax.broadcasted_iota(jnp.int32, (tile, keys_n), 1)
        allowed = (k <= p) & (k < count_ref[f])
        scores = jnp.where(allowed, scores, -1e30)
        exponent = jnp.exp(scores - jnp.max(scores, axis=-1, keepdims=True))
        weights = exponent * (1.0 / jnp.sum(exponent, axis=-1, keepdims=True))
        weights_b = weights.astype(BF16)
        attn_ref[f, at, :] = jnp.dot(weights_b, values, preferred_element_type=F32).astype(BF16)
        d_weights = lax.dot_general(upstream, values, over, preferred_element_type=F32)
        center = jnp.sum(weights * d_weights, axis=-1, keepdims=True)
        d_scores = (weights * (d_weights - center) * scale).astype(BF16)
        dpr[f, at, 0:HD] = jnp.dot(d_scores, keys, preferred_element_type=F32).astype(BF16)
        d_values = lax.dot_general(weights_b, upstream, down, preferred_element_type=F32)
        d_keys = lax.dot_general(d_scores, query, down, preferred_element_type=F32)
        old = i * tile
        if i:
            dv_acc[0:old, :] += d_values[0:old]
            dk_acc[0:old, :] += d_keys[0:old]
        dv_acc[at, :] = d_values[old:]
        dk_acc[at, :] = d_keys[old:]

    def attended(f):
        dpr[f, :, HD : 2 * HD] = dk_acc[...].astype(BF16)
        dpr[f, :, 2 * HD : 3 * HD] = dv_acc[...].astype(BF16)

    def back(f, i):
        rows = dpr[f, i * tile : (i + 1) * tile, :]
        term = lax.dot_general(rows, wgt[...], (((1,), (1,)), ((), ())), preferred_element_type=F32)
        part[f, i * per : (i + 1) * per] = term.astype(BF16).reshape(per, local_len, width)
        for k in range(per // 2):
            mx_copy(f, i * per // 2 + k).start()

    def turned(f):
        dpt[:, f * length : (f + 1) * length] = dpr[f].T

    def grad(j):
        cols = slice(j * 2 * LANES, (j + 1) * 2 * LANES)
        got = jnp.zeros((dpt.shape[0], 2 * LANES), F32)
        for f in range(seqs):
            rows = gat[f, :, :, cols].reshape(length, 2 * LANES)
            got += jnp.dot(dpt[:, f * length : (f + 1) * length], rows, preferred_element_type=F32)
        for k in range(2):
            grad_ref[2 * j + k] = got[:, k * LANES : (k + 1) * LANES].astype(BF16)

    def sequence_work(f):
        work = [functools.partial(project, f, i) for i in range(tiles)]
        work += [functools.partial(attend, f, i) for i in range(tiles)]
        work += [functools.partial(attended, f)]
        return work + [functools.partial(back, f, i) for i in range(tiles)]

    def interleave(events, work):
        done = 0
        for n, event in enumerate(events):
            event()
            upto = (n + 1) * len(work) // len(events)
            for item in work[done:upto]:
                item()
            done = upto

    ag_begin(0)
    for c in range(3):
        wgt[:, c * HD : (c + 1) * HD] = weight_ref[c]
    events = ag_events(0)
    for event in events[:-4]:
        event()
    ag_begin(1)
    for event in events[-4:]:
        event()
    ag_end(0)
    interleave(ag_events(1), sequence_work(0))
    ag_end(1)
    interleave(rs_events(0), [functools.partial(turned, 0)] + sequence_work(1))
    rs_end(0)
    interleave(rs_events(1), [functools.partial(turned, 1)] + [functools.partial(grad, j) for j in range(width // (2 * LANES))])
    rs_end(1)
    for f in range(seqs):
        for d in range(2):
            for e in range(hops):
                ag_copy(f, d, e).wait_send()
                rs_copy(f, d, e).wait_send()
        for n in range(1 + 2 * hops):
            sb_copy(f, n).wait_send()
        for k in range(nz):
            mx_copy(f, k).wait_send()


def layer(ns, seqs, count, normed, inputs, ufactor, ugain, weight, dout):
    rows, width = normed.shape
    local_len = rows // seqs
    length = ns * local_len
    nz = ns // 2
    hops = nz - 1
    vmem = pl.BlockSpec(memory_space=pltpu.VMEM)
    cols = 3 * HD
    return pl.pallas_call(
        functools.partial(layer_kernel, ns),
        out_shape=(
            jax.ShapeDtypeStruct((seqs, length, HD), BF16),
            jax.ShapeDtypeStruct((width // LANES, cols, LANES), BF16),
            jax.ShapeDtypeStruct((rows, width), BF16),
            jax.ShapeDtypeStruct((1, width), F32),
        ),
        in_specs=[pl.BlockSpec(memory_space=pltpu.SMEM)] + [vmem] * 6,
        out_specs=[vmem] * 4,
        scratch_shapes=[
            pltpu.VMEM((seqs, ns, local_len, width), BF16),
            pltpu.VMEM((seqs, length, cols), BF16),
            pltpu.VMEM((seqs, length, cols), BF16),
            pltpu.VMEM((cols, seqs * length), BF16),
            pltpu.VMEM((width, cols), BF16),
            pltpu.VMEM((seqs, ns, local_len, width), BF16),
            pltpu.VMEM((seqs, nz, local_len, width), BF16),
            pltpu.VMEM((seqs, 2, hops, local_len // 2, width), BF16),
            pltpu.VMEM((length, HD), F32),
            pltpu.VMEM((length, HD), F32),
        ]
        + [pltpu.SemaphoreType.DMA((seqs, 2, hops))] * 2
        + [pltpu.SemaphoreType.DMA((seqs, 1 + 2 * hops))] * 2
        + [pltpu.SemaphoreType.DMA((seqs, nz))] * 2
        + [pltpu.SemaphoreType.DMA((seqs, 2, hops))] * 2,
        compiler_params=pltpu.CompilerParams(
            collective_id=1, has_side_effects=True, vmem_limit_bytes=VMEM_LIMIT
        ),
        name="layer",
    )(count, normed, inputs, ufactor, ugain, weight, dout)


def home_kernel(
    ng, ns, nd, cap, ids_ref, val_ref, hidden_ref, igain_ref, dinputs_ref, uterms_ref, grad_ref,
    dhidden_ref, gains_ref, full_ref,
    stack, out, arr, gin, tin, tin2, tsum,
    row_send, row_recv, gr_send, gr_recv, gg_send, gg_recv, t_send, t_recv, u_send, u_recv,
):
    owners, msg = ns * nd, cap * Q
    per = LANES // msg
    groups = owners // per
    items, width = hidden_ref.shape
    part = width // Q
    nr = ng * nd
    seq, dp, grp = lax.axis_index("seq"), lax.axis_index("dp"), lax.axis_index("grp")
    me = seq * nd + dp
    rep = grp * nd + dp
    barrier = pltpu.get_barrier_semaphore()

    def rep_peer(index):
        return {"grp": index // nd, "dp": lax.rem(index, nd)}

    @pl.loop(1, owners)
    def _(i):
        greet(barrier, plane_peer(lax.rem(me + i, owners), nd))

    @pl.loop(nd, nr)
    def _(i):
        greet(barrier, rep_peer(lax.rem(grp * nd + i, nr)))

    owner_row, rank_row, base_row = slots(ids_ref, cap)
    for q in range(Q):
        stack[q * LANES : (q + 1) * LANES, :] = dinputs_ref[:, q * part : (q + 1) * part]
    pl.semaphore_wait(barrier, owners - 1 + nr - nd)

    my_group = me // per
    gchunk = width // LANES // nr

    def grads_out(i):
        peer = lax.rem(rep + i, nr)
        remote(grad_ref.at[pl.ds(peer * gchunk, gchunk)], gin.at[rep], gr_send, gr_recv, rep_peer(peer)).start()

    for step in range(groups):
        turn = (step + 1) // 2 if step % 2 else groups - step // 2
        g = lax.rem(my_group + turn, groups)
        rows = iota((LANES, LANES), 0) + (g * LANES).astype(F32)
        place = jnp.concatenate([onehot(rows == base_row + q) for q in range(Q)], axis=1)
        sent = jnp.dot(place, stack[...], preferred_element_type=F32).astype(BF16)
        out[pl.ds(g * per, per)] = sent.reshape(per, msg, part)
        for k in range(per):
            peer = g * per + k

            @pl.when(peer != me)
            def _():
                remote(out.at[peer], arr.at[me], row_send, row_recv, plane_peer(peer, nd)).start()

        for i in range(1 + step * (nr - 1) // groups, 1 + (step + 1) * (nr - 1) // groups):
            grads_out(i)

    arr[me] = out[me]
    gin[rep] = grad_ref[pl.ds(rep * gchunk, gchunk)]
    remote(
        grad_ref.at[pl.ds(0, (nr - 1) * gchunk)], grad_ref.at[pl.ds(0, (nr - 1) * gchunk)], gr_send, gr_recv, rep_peer(rep)
    ).wait()
    got = gin[0].astype(F32)
    for i in range(1, nr):
        got += gin[i].astype(F32)
    mine = pl.ds(rep * gchunk, gchunk)
    full_ref[mine] = got.astype(BF16)

    @pl.loop(1, nr)
    def _(i):
        remote(full_ref.at[mine], full_ref.at[mine], gg_send, gg_recv, rep_peer(lax.rem(rep + i, nr))).start()

    hidden = hidden_ref[...].astype(F32)
    factor = lax.rsqrt(jnp.mean(hidden * hidden, axis=-1, keepdims=True) + EPS)
    remote(
        out.at[pl.ds(0, owners - 1)], arr.at[pl.ds(0, owners - 1)], row_send, row_recv, plane_peer(me, nd)
    ).wait()
    took = jnp.zeros((Q * items, part), F32)
    for g in range(groups):
        pick = onehot(iota((Q * items, LANES), 0) == val_ref[g].astype(F32))
        rows = arr[g * per : (g + 1) * per].reshape(LANES, part)
        took += jnp.dot(pick, rows, preferred_element_type=F32)
    center = jnp.zeros((items, 1), F32)
    terms = []
    for q in range(Q):
        cols = slice(q * part, (q + 1) * part)
        h = hidden_ref[:, cols].astype(F32)
        d = took[q * items : (q + 1) * items]
        center += jnp.sum(igain_ref[:, cols] * d * h, axis=-1, keepdims=True)
        tsum[q : q + 1, :] = jnp.sum(d * h * factor, axis=0, keepdims=True)
        tsum[Q + q : Q + q + 1, :] = uterms_ref[:, cols]
    center = center / width
    tin[seq] = tsum[...]

    @pl.loop(1, ns)
    def _(i):
        remote(tsum, tin.at[seq], t_send, t_recv, {"seq": lax.rem(seq + i, ns)}).start()

    for q in range(Q):
        cols = slice(q * part, (q + 1) * part)
        h = hidden_ref[:, cols].astype(F32)
        d = took[q * items : (q + 1) * items]
        dhidden_ref[:, cols] = (factor * igain_ref[:, cols] * d - h * (factor * factor * factor * center)).astype(BF16)

    remote(tin.at[pl.ds(0, ns - 1)], tin.at[pl.ds(0, ns - 1)], t_send, t_recv, {"seq": seq}).wait()
    total = tin[0]
    for i in range(1, ns):
        total = total + tin[i]
    tin2[rep] = total

    @pl.loop(1, nr)
    def _(i):
        remote(tin2.at[rep], tin2.at[rep], u_send, u_recv, rep_peer(lax.rem(rep + i, nr))).start()

    remote(tin2.at[pl.ds(0, nr - 1)], tin2.at[pl.ds(0, nr - 1)], u_send, u_recv, rep_peer(rep)).wait()
    total = tin2[0]
    for i in range(1, nr):
        total = total + tin2[i]
    gains_ref[...] = total
    remote(
        full_ref.at[pl.ds(0, (nr - 1) * gchunk)], full_ref.at[pl.ds(0, (nr - 1) * gchunk)], gg_send, gg_recv, rep_peer(rep)
    ).wait()


def home(ng, ns, nd, cap, ids, val, hidden, igain, dinputs, uterms, grads):
    items, width = hidden.shape
    owners, msg = ns * nd, cap * Q
    nr = ng * nd
    part = width // Q
    gchunk = width // LANES // nr
    vmem = pl.BlockSpec(memory_space=pltpu.VMEM)
    return pl.pallas_call(
        functools.partial(home_kernel, ng, ns, nd, cap),
        out_shape=(
            jax.ShapeDtypeStruct((items, width), BF16),
            jax.ShapeDtypeStruct((2 * Q, part), F32),
            jax.ShapeDtypeStruct(grads.shape, BF16),
        ),
        in_specs=[vmem] * 7,
        out_specs=[vmem] * 3,
        scratch_shapes=[
            pltpu.VMEM((Q * LANES, part), BF16),
            pltpu.VMEM((owners, msg, part), BF16),
            pltpu.VMEM((owners, msg, part), BF16),
            pltpu.VMEM((nr, gchunk, grads.shape[1], LANES), BF16),
            pltpu.VMEM((ns, 2 * Q, part), F32),
            pltpu.VMEM((nr, 2 * Q, part), F32),
            pltpu.VMEM((2 * Q, part), F32),
        ]
        + [pltpu.SemaphoreType.DMA] * 10,
        compiler_params=pltpu.CompilerParams(
            collective_id=2, has_side_effects=True, vmem_limit_bytes=VMEM_LIMIT
        ),
        name="home",
    )(ids, val, hidden, igain, dinputs, uterms, grads)


def local(
    item_hidden, item_gain, slot_owner, slot_row, seq_count, user_gain, query_key_value_weight, d_out
):
    ng, ns, nd = (lax.axis_size(a) for a in ("grp", "seq", "dp"))
    seqs, local_len, _ = slot_owner.shape
    width = item_hidden.shape[1]
    cap = seqs * max(2, 2 * local_len // (ns * nd))
    ids = jnp.stack([slot_owner.reshape(-1), slot_row.reshape(-1)])
    igain, ugain = item_gain.reshape(1, width), user_gain.reshape(1, width)
    normed, inputs, ufactor, val = fetch(ns, nd, cap, ids, item_hidden, igain, ugain)
    attn, grads, dinputs, uterms = layer(
        ns, seqs, seq_count, normed, inputs, ufactor, ugain, query_key_value_weight, d_out
    )
    d_hidden, gains, full = home(ng, ns, nd, cap, ids, val, item_hidden, igain, dinputs, uterms, grads)
    full = full.reshape(width // LANES, 3, HD, LANES).transpose(1, 0, 3, 2).reshape(3, width, HD)
    return (attn, d_hidden, full.astype(F32), gains[Q:].reshape(width), gains[:Q].reshape(width))


def solution(mesh):
    in_specs = (
        P(("grp", "seq", "dp"), None),
        P(),
        P(("grp", "dp"), "seq", None),
        P(("grp", "dp"), "seq"),
        P(("grp", "dp")),
        P(),
        P(None, None, "seq"),
        P(("grp", "dp"), None, "seq"),
    )
    out_specs = (
        P(("grp", "dp"), None, "seq"),
        P(("grp", "seq", "dp"), None),
        P(None, None, "seq"),
        P(),
        P(),
    )
    return jax.shard_map(local, mesh=mesh, in_specs=in_specs, out_specs=out_specs, check_vma=False)
```

time: 453 us -> 253 us (0.56)
  the two profiles are of different devices: /device:TPU:1 before, /device:TPU:88 now
where the time goes in v1:
time: 253 us
  Pallas kernels  239 us (94%)
  local copies, waits for them, and re-layouts  9.47 us (4%)
  other arithmetic  3.68 us (1%)
    pallas_call x1, Pallas kernels, layer(): pl.pallas_call(functools.partial(layer_kernel, ns), out_shape=(jax.ShapeD...  112 us
    pallas_call x1, Pallas kernels, home(): pl.pallas_call(functools.partial(home_kernel, ng, ns, nd, cap), out_shape...  85.7 us
    pallas_call x1, Pallas kernels, fetch(): pl.pallas_call(functools.partial(fetch_kernel, ns, nd, cap), out_shape=(j...  41.1 us
    unnamed x6, local copies, waits for them, and re-layouts  6.26 us

profile of v1, /device:TPU:88, one launch (start us, length us, event | category | flops | bytes accessed | tf_op | source)
XLA Modules:
  0.0 253.0 jit_solution(6898794664205166190)
XLA Ops:
  0.6 0.5 broadcast.3
  1.1 1.3 reduce.3
  2.5 0.1 stack_reshape.6
  2.6 0.8 stack_reshape.7
  3.3 0.6 pad_add_fusion.ids_ref
  3.9 41.1 %fetch.1 = (bf16[128,2048]{1,0:T(8,128)(2,1)}, bf16[128,2048]{1,0:T(8,128)(2,1)}, f32[128,1]{1,0:T(8,128)}, s32[8,1,128]{2,1,0:T(1,128)}) custom-call(s32[2,128]{1,0:T(2,128)} %pad_add_fusion.ids_ref, bf16[128,2048]{1,0:T(8,128)(2,1)} %hidden_ref.3, f32[1,2048]{1,0:T(1,128)} %bitcast.18, f32[1,2048]{1,0:T(1,128)} %bitcast.16), custom_call_target="tpu_custom_call" | custom-call | tf_op jit(solution)/shard_map/fetch/pallas_call | solution.py:147
  45.0 112.4 %layer.1 = (bf16[2,1024,128]{2,1,0:T(8,128)(2,1)}, bf16[16,384,128]{2,1,0:T(8,128)(2,1)}, bf16[128,2048]{1,0:T(8,128)(2,1)}, f32[1,2048]{1,0:T(1,128)}) custom-call(s32[2]{0:T(128)} %count_ref.1, bf16[128,2048]{1,0:T(8,128)(2,1)} %get-tuple-element.16.normed_ref, bf16[128,2048]{1,0:T(8,128)(2,1)} %get-tuple-element.17.inputs_ref, ...), custom_call_target="tpu_custom_call" | custom-call | tf_op jit(solution)/shard_map/layer/pallas_call | solution.py:439
  157.4 85.7 %home.1 = (bf16[128,2048]{1,0:T(8,128)(2,1)}, f32[8,512]{1,0:T(8,128)}, bf16[16,384,128]{2,1,0:T(8,128)(2,1)}) custom-call(s32[2,128]{1,0:T(2,128)} %pad_add_fusion.ids_ref, s32[8,1,128]{2,1,0:T(1,128)} %get-tuple-element.20.val_ref, bf16[128,2048]{1,0:T(8,128)(2,1)} %hidden_ref.3, f32[1,2048]{1,0:T(1,128)} %bitcast.19, ...), custom_call_target="tpu_custom_call" | custom-call | tf_op jit(solution)/shard_map/home/pallas_call | solution.py:603
  243.2 0.8 slice_bitcast_fusion
  244.0 0.6 copy.15
  244.6 0.6 copy.14
  245.2 1.8 convert_bitcast_fusion
  246.9 2.4 copy.13
  249.3 1.9 copy.18
  251.2 1.9 copy.19

commit v2 on v1

v2 whole, which is shorter than its diff:
```python
import functools
import math

import jax
import jax.numpy as jnp
from jax import lax
from jax.experimental import pallas as pl
from jax.experimental.pallas import tpu as pltpu
from jax.sharding import PartitionSpec as P

HD = 128
LANES = 128
Q = 8
EPS = 1e-05
MESH = pl.DeviceIdType.MESH
F32, BF16 = jnp.float32, jnp.bfloat16
VMEM_LIMIT = 60 * 2**20


def iota(shape, dim):
    return lax.broadcasted_iota(jnp.int32, shape, dim).astype(F32)


def onehot(mask):
    return jnp.where(mask, 1.0, 0.0).astype(BF16)


def column(row):
    return jnp.broadcast_to(row, (LANES, LANES)).T


def plane_peer(index, nd):
    return {"seq": index // nd, "dp": lax.rem(index, nd)}


def greet(barrier, device):
    pl.semaphore_signal(barrier, inc=1, device_id=device, device_id_type=MESH)


def remote(src, dst, send, recv, device):
    return pltpu.make_async_remote_copy(
        src_ref=src, dst_ref=dst, send_sem=send, recv_sem=recv, device_id=device, device_id_type=MESH
    )


def slots(owner_ref, cap, f):
    own = owner_ref[f].astype(F32)
    length = own.shape[1]
    owner_row = jnp.concatenate([own, own], axis=1)
    owner = jnp.broadcast_to(owner_row, (LANES, LANES))
    this = iota((LANES, LANES), 1)
    this = jnp.where(this >= length, this - length, this)
    earlier = (owner == owner.T) & (iota((LANES, LANES), 0) < this)
    rank_row = jnp.sum(jnp.where(earlier, 1.0, 0.0), axis=0, keepdims=True)
    return owner_row, rank_row, (owner_row * cap + rank_row) * Q


def main_kernel(
    ng, ns, nd, cap,
    count_ref, owner_ref, row_ref, hidden_ref, igain_ref, ugain_ref, weight_ref, dout_ref,
    attn_ref, dhidden_ref, full_ref, ugrad_ref, igrad_ref,
    req, reqr, val, table, out, arr, stack, back_out, back_arr,
    inputs, ufactor, dinputs, uterms,
    gat, prj, dpr, dpt, wgt, part, mix, ring, dk_acc, dv_acc,
    grad_out, gin, tmine, tin, tmid,
    id_send, id_recv, row_send, row_recv, bk_send, bk_recv,
    ag_send, ag_recv, sb_send, sb_recv, mx_send, mx_recv, rs_send, rs_recv,
    gr_send, gr_recv, gg_send, gg_recv, t_send, t_recv, u_send, u_recv,
):
    seqs, _, local_len, width = gat.shape
    items = hidden_ref.shape[0]
    length = ns * local_len
    owners, msg = ns * nd, cap * Q
    per_g = LANES // msg
    groups = owners // per_g
    piece = width // Q
    nr = ng * nd
    nz = ns // 2
    half = nz // 2
    hops = 2 * half - 1
    hl = local_len // 2
    per = 4
    tile = per * local_len
    tiles = ns // per
    seq, dp, grp = lax.axis_index("seq"), lax.axis_index("dp"), lax.axis_index("grp")
    me = seq * nd + dp
    rep = grp * nd + dp
    z, core = seq // 2, lax.rem(seq, 2)
    sib_index = seq + 1 - 2 * core
    sib = {"seq": sib_index}
    ahead = ({"seq": lax.rem(seq + 2, ns)}, {"seq": lax.rem(seq + ns - 2, ns)})
    scale = 1.0 / math.sqrt(HD)
    my_group = me // per_g

    def rep_peer(index):
        return {"grp": index // nd, "dp": lax.rem(index, nd)}

    def turn_of(step):
        turn = (step + 1) // 2 if step % 2 else groups - step // 2
        return lax.rem(my_group + turn, groups)

    barrier = pltpu.get_barrier_semaphore()

    @pl.loop(1, owners)
    def _(i):
        greet(barrier, plane_peer(lax.rem(me + i, owners), nd))

    @pl.loop(nd, nr)
    def _(i):
        greet(barrier, rep_peer(lax.rem(grp * nd + i, nr)))

    lane = lax.broadcasted_iota(jnp.int32, (LANES, LANES), 1)
    slot_in = ((lane % msg) // Q).astype(F32)
    piece_of = (lane[0:1, :] % Q).astype(F32)
    places = []
    for f in range(seqs):
        owner_row, rank_row, base_row = slots(owner_ref, cap, f)
        places.append(base_row)
        want = row_ref[f : f + 1, :].astype(F32) + 1.0
        row_col = column(jnp.concatenate([want, jnp.zeros_like(want)], axis=1))
        wanted = jnp.where(column(rank_row) == slot_in, row_col, 0.0).astype(BF16)
        names = onehot(iota((owners, LANES), 0) == owner_row)
        asked = jnp.dot(names, wanted, preferred_element_type=F32)
        asked = jnp.where(asked > 0.5, asked - 1.0 + piece_of * items, -1.0).astype(jnp.int32)
        for o in range(owners):
            req[o, f : f + 1, :] = asked[o : o + 1, :]

    pl.semaphore_wait(barrier, owners - 1 + nr - nd)

    @pl.loop(1, owners)
    def _(i):
        peer = lax.rem(me + i, owners)
        remote(req.at[peer], reqr.at[me], id_send, id_recv, plane_peer(peer, nd)).start()

    reqr[me] = req[me]
    hidden = hidden_ref[...].astype(F32)
    ifactor = lax.rsqrt(jnp.mean(hidden * hidden, axis=-1, keepdims=True) + EPS)
    for q in range(Q):
        cols = slice(q * piece, (q + 1) * piece)
        table[q * items : (q + 1) * items, :] = (
            hidden_ref[:, cols].astype(F32) * ifactor * igain_ref[:, cols]
        ).astype(BF16)
    remote(
        req.at[pl.ds(0, owners - 1)], reqr.at[pl.ds(0, owners - 1)], id_send, id_recv, plane_peer(me, nd)
    ).wait()

    def send_group(src, dst, f, g, send, recv):
        for k in range(per_g):
            peer = g * per_g + k

            @pl.when(peer != me)
            def _():
                remote(src.at[f, peer], dst.at[f, me], send.at[f], recv.at[f], plane_peer(peer, nd)).start()

    def all_groups(src, dst, f, send, recv):
        some = pl.ds(0, owners - 1)
        return remote(src.at[f, some], dst.at[f, some], send.at[f], recv.at[f], plane_peer(me, nd))

    lane_group = lax.broadcasted_iota(jnp.int32, (1, LANES), 1) // msg

    def fetch(f, step):
        g = turn_of(step)
        ids = jnp.zeros((1, LANES), jnp.int32)
        for k in range(per_g):
            ids = jnp.where(lane_group == k, reqr[g * per_g + k][f : f + 1, :], ids)
        val[f, g] = ids
        col = column(ids.astype(F32))
        pick = jnp.concatenate([onehot(col == iota((LANES, LANES), 1) + q * items) for q in range(Q)], axis=1)
        picked = jnp.dot(pick, table[...], preferred_element_type=F32).astype(BF16)
        out[f, pl.ds(g * per_g, per_g)] = picked.reshape(per_g, msg, piece)
        send_group(out, arr, f, g, row_send, row_recv)

    def place(f):
        arr[f, me] = out[f, me]
        base_col = column(places[f])[0:local_len]
        all_groups(out, arr, f, row_send, row_recv).wait_recv()
        arrived = arr[f].reshape(owners * msg, piece)
        total = jnp.zeros((local_len, 1), F32)
        for q in range(Q):
            put = jnp.concatenate(
                [onehot(iota((local_len, LANES), 1) + t * LANES == base_col + q) for t in range(groups)], axis=1
            )
            rows = jnp.dot(put, arrived, preferred_element_type=F32)
            inputs[f, :, q * piece : (q + 1) * piece] = rows.astype(BF16)
            total += jnp.sum(rows * rows, axis=-1, keepdims=True)
        factor = lax.rsqrt(total / width + EPS)
        ufactor[f] = factor
        gat[f, seq] = (inputs[f].astype(F32) * factor * ugain_ref[...]).astype(BF16)

    def give_back(f, step):
        if step == 0:
            for q in range(Q):
                stack[f, q * local_len : (q + 1) * local_len, :] = dinputs[f, :, q * piece : (q + 1) * piece]
        g = turn_of(step)
        rows = iota((LANES, LANES), 0) + (g * LANES).astype(F32)
        second = jnp.where(iota((1, LANES), 1) >= local_len, 1.0, 0.0)
        put = jnp.concatenate([onehot(rows == places[f] + (2.0 * t + second)) for t in range(Q // 2)], axis=1)
        sent = jnp.dot(put, stack[f], preferred_element_type=F32).astype(BF16)
        back_out[f, pl.ds(g * per_g, per_g)] = sent.reshape(per_g, msg, piece)
        send_group(back_out, back_arr, f, g, bk_send, bk_recv)

    def taken(f):
        back_arr[f, me] = back_out[f, me]
        all_groups(back_out, back_arr, f, bk_send, bk_recv).wait_recv()
        pick = jnp.concatenate([onehot(iota((Q * items, LANES), 0) == val[f, g].astype(F32)) for g in range(groups)], axis=1)
        return jnp.dot(pick, back_arr[f].reshape(owners * msg, piece), preferred_element_type=F32)

    def ag_place(f, d, e, origin):
        far = e // 2
        h = d if e == hops - 1 else e % 2
        block = lax.rem(origin + (ns - 2 * far if d == 0 else 2 * far), ns)
        return gat.at[f, block, pl.ds(h * hl, hl)]

    def ag_copy(f, d, e):
        ref = ag_place(f, d, e, seq)
        return remote(ref, ref, ag_send.at[f, d, e], ag_recv.at[f, d, e], ahead[d])

    def ag_arrival(f, d, e, at):
        behind = lax.rem(at + (ns - 2 if d == 0 else 2), ns)
        return ag_place(f, d, e, behind)

    def ag_wait(f, d, e):
        ref = ag_arrival(f, d, e, seq)
        remote(ref, ref, ag_send.at[f, d, e], ag_recv.at[f, d, e], ahead[d]).wait_recv()

    def sb_copy(f, n):
        ref = gat.at[f, seq] if n == 0 else ag_arrival(f, (n - 1) % 2, (n - 1) // 2, seq)
        return remote(ref, ref, sb_send.at[f, n], sb_recv.at[f, n], sib)

    def sb_wait(f, n):
        ref = gat.at[f, sib_index] if n == 0 else ag_arrival(f, (n - 1) % 2, (n - 1) // 2, sib_index)
        remote(ref, ref, sb_send.at[f, n], sb_recv.at[f, n], sib).wait_recv()

    def ag_begin(f):
        for e in range(min(2, hops)):
            for d in range(2):
                ag_copy(f, d, e).start()
        sb_copy(f, 0).start()

    def ag_event(f, d, e):
        ag_wait(f, d, e)
        if e + 2 < hops - 1:
            ag_copy(f, d, e + 2).start()
        elif e + 2 == hops - 1 + d:
            ag_copy(f, d, hops - 1).start()
        sb_copy(f, 1 + 2 * e + d).start()

    def ag_events(f):
        return [functools.partial(ag_event, f, d, e) for e in range(hops) for d in range(2)]

    def ag_end(f):
        for n in range(1 + 2 * hops):
            sb_wait(f, n)

    order = [(half, None)] + [(t, h) for t in range(half - 1, 0, -1) for h in range(2)]

    def rs_what(d, i):
        t, h = order[i]
        return t, d if h is None else h

    def chip(d, t):
        return lax.rem(z + (t if d == 0 else nz - t), nz)

    def rs_copy(f, d, i):
        t, h = rs_what(d, i)
        return remote(
            mix.at[f, chip(d, t), pl.ds(h * hl, hl)], ring.at[f, d, i], rs_send.at[f, d, i], rs_recv.at[f, d, i], ahead[d]
        )

    def mx_copy(f, k):
        return remote(part.at[f, 2 * k + 1 - core], mix.at[f, k], mx_send.at[f, k], mx_recv.at[f, k], sib)

    def own_sum(f, k):
        mix[f, k] = (mix[f, k].astype(F32) + part[f, 2 * k + core].astype(F32)).astype(BF16)

    def rs_source(d, i):
        t, h = rs_what(d, i)
        for j in range(len(order)):
            if rs_what(d, j) == (t + 1, h):
                return j
        return None

    def rs_own(f, t):
        own_sum(f, chip(0, t))
        if 0 < t < half:
            own_sum(f, chip(1, t))
        for d in range(2):
            for i in range(len(order)):
                if rs_what(d, i)[0] == t and rs_source(d, i) is None:
                    rs_copy(f, d, i).start()

    def rs_start(f):
        for k in range(nz):
            mx_copy(f, k).wait_recv()
        rs_own(f, half)
        rs_own(f, half - 1)

    def rs_event(f, d, j):
        rs_copy(f, d, j).wait_recv()
        t, h = rs_what(d, j)
        if t == 1:
            return
        for i in range(len(order)):
            if rs_what(d, i) == (t - 1, h):
                rows = pl.ds(h * hl, hl)
                k = chip(d, t - 1)
                mix[f, k, rows] = (mix[f, k, rows].astype(F32) + ring[f, d, j].astype(F32)).astype(BF16)
                rs_copy(f, d, i).start()

    def rs_events(f):
        events = [functools.partial(rs_own, f, t) for t in range(half - 2, -1, -1)]
        return events + [functools.partial(rs_event, f, d, j) for j in range(len(order)) for d in range(2)]

    def rs_end(f):
        total = mix[f, z].astype(F32)
        for h in range(2):
            rows = slice(h * hl, (h + 1) * hl)
            got = total[rows]
            for d in range(2):
                for i in range(len(order)):
                    if rs_what(d, i) == (1, h):
                        got = got + ring[f, d, i].astype(F32)
            values = inputs[f, rows, :].astype(F32)
            factor = ufactor[f, rows, :]
            term = jnp.sum(got * values * factor, axis=0, keepdims=True)
            if f == 0 and h == 0:
                uterms[...] = term
            else:
                uterms[...] += term
            weighted = ugain_ref[...] * got
            center = jnp.mean(weighted * values, axis=-1, keepdims=True)
            dinputs[f, rows, :] = (factor * weighted - values * (factor * factor * factor * center)).astype(BF16)

    def project(f, i):
        rows = gat[f, i * per : (i + 1) * per].reshape(tile, width)
        prj[f, i * tile : (i + 1) * tile, :] = jnp.dot(rows, wgt[...], preferred_element_type=F32).astype(BF16)

    def attend(f, i):
        keys_n = (i + 1) * tile
        at = slice(i * tile, (i + 1) * tile)
        query = prj[f, at, 0:HD]
        keys = prj[f, 0:keys_n, HD : 2 * HD]
        values = prj[f, 0:keys_n, 2 * HD : 3 * HD]
        upstream = dout_ref[f, at, :]
        over = (((1,), (1,)), ((), ()))
        down = (((0,), (0,)), ((), ()))
        scores = lax.dot_general(query, keys, over, preferred_element_type=F32) * scale
        p = lax.broadcasted_iota(jnp.int32, (tile, keys_n), 0) + i * tile
        k = lax.broadcasted_iota(jnp.int32, (tile, keys_n), 1)
        allowed = (k <= p) & (k < count_ref[f])
        scores = jnp.where(allowed, scores, -1e30)
        exponent = jnp.exp(scores - jnp.max(scores, axis=-1, keepdims=True))
        weights = exponent * (1.0 / jnp.sum(exponent, axis=-1, keepdims=True))
        weights_b = weights.astype(BF16)
        attn_ref[f, at, :] = jnp.dot(weights_b, values, preferred_element_type=F32).astype(BF16)
        d_weights = lax.dot_general(upstream, values, over, preferred_element_type=F32)
        center = jnp.sum(weights * d_weights, axis=-1, keepdims=True)
        d_scores = (weights * (d_weights - center) * scale).astype(BF16)
        dpr[f, at, 0:HD] = jnp.dot(d_scores, keys, preferred_element_type=F32).astype(BF16)
        d_values = lax.dot_general(weights_b, upstream, down, preferred_element_type=F32)
        d_keys = lax.dot_general(d_scores, query, down, preferred_element_type=F32)
        old = i * tile
        if i:
            dv_acc[0:old, :] += d_values[0:old]
            dk_acc[0:old, :] += d_keys[0:old]
        dv_acc[at, :] = d_values[old:]
        dk_acc[at, :] = d_keys[old:]

    def attended(f):
        dpr[f, :, HD : 2 * HD] = dk_acc[...].astype(BF16)
        dpr[f, :, 2 * HD : 3 * HD] = dv_acc[...].astype(BF16)

    def back(f, i):
        rows = dpr[f, i * tile : (i + 1) * tile, :]
        term = lax.dot_general(rows, wgt[...], (((1,), (1,)), ((), ())), preferred_element_type=F32)
        part[f, i * per : (i + 1) * per] = term.astype(BF16).reshape(per, local_len, width)
        for k in range(per // 2):
            mx_copy(f, i * per // 2 + k).start()

    def turned(f):
        dpt[:, f * length : (f + 1) * length] = dpr[f].T

    def grad(j):
        cols = slice(j * 2 * LANES, (j + 1) * 2 * LANES)
        got = jnp.zeros((dpt.shape[0], 2 * LANES), F32)
        for f in range(seqs):
            rows = gat[f, :, :, cols].reshape(length, 2 * LANES)
            got += jnp.dot(dpt[:, f * length : (f + 1) * length], rows, preferred_element_type=F32)
        for k in range(2):
            grad_out[2 * j + k] = got[:, k * LANES : (k + 1) * LANES].astype(BF16)

    gchunk = width // LANES // nr
    gmine = pl.ds(rep * gchunk, gchunk)
    gsome = pl.ds(0, (nr - 1) * gchunk)

    def grads_start():
        @pl.loop(1, nr)
        def _(i):
            peer = lax.rem(rep + i, nr)
            remote(grad_out.at[pl.ds(peer * gchunk, gchunk)], gin.at[rep], gr_send, gr_recv, rep_peer(peer)).start()

        gin[rep] = grad_out[gmine]

    def grads_sum():
        remote(grad_out.at[gsome], grad_out.at[gsome], gr_send, gr_recv, rep_peer(rep)).wait_recv()
        got = gin[0].astype(F32)
        for i in range(1, nr):
            got += gin[i].astype(F32)
        full_ref[gmine] = got.astype(BF16)

        @pl.loop(1, nr)
        def _(i):
            remote(full_ref.at[gmine], full_ref.at[gmine], gg_send, gg_recv, rep_peer(lax.rem(rep + i, nr))).start()

    def gain_start(n):
        tin[n, seq] = tmine[n]

        @pl.loop(1, ns)
        def _(i):
            remote(tmine.at[n], tin.at[n, seq], t_send.at[n], t_recv.at[n], {"seq": lax.rem(seq + i, ns)}).start()

    def gain_turn(n):
        some = pl.ds(0, ns - 1)
        remote(tin.at[n, some], tin.at[n, some], t_send.at[n], t_recv.at[n], {"seq": seq}).wait()
        total = tin[n, 0]
        for i in range(1, ns):
            total = total + tin[n, i]
        tmid[n, rep] = total

        @pl.loop(1, nr)
        def _(i):
            there = tmid.at[n, rep]
            remote(there, there, u_send.at[n], u_recv.at[n], rep_peer(lax.rem(rep + i, nr))).start()

    def gain_end(n, to_ref):
        some = pl.ds(0, nr - 1)
        remote(tmid.at[n, some], tmid.at[n, some], u_send.at[n], u_recv.at[n], rep_peer(rep)).wait()
        total = tmid[n, 0]
        for i in range(1, nr):
            total = total + tmid[n, i]
        for q in range(Q):
            to_ref[:, q * piece : (q + 1) * piece] = total[q : q + 1, :]

    def sequence_work(f):
        work = [functools.partial(project, f, i) for i in range(tiles)]
        work += [functools.partial(attend, f, i) for i in range(tiles)]
        work += [functools.partial(attended, f)]
        return work + [functools.partial(back, f, i) for i in range(tiles)]

    def interleave(events, work):
        done = 0
        for n, event in enumerate(events):
            event()
            upto = (n + 1) * len(work) // len(events)
            for item in work[done:upto]:
                item()
            done = upto

    for f in range(seqs):
        for step in range(groups):
            fetch(f, step)
    for c in range(3):
        wgt[:, c * HD : (c + 1) * HD] = weight_ref[c]
    place(0)
    ag_begin(0)
    events = ag_events(0)
    first, last = 2 * hops // 4, 2 * hops // 2
    interleave(events[:first], [])
    place(1)
    interleave(events[first:last], [])
    ag_begin(1)
    interleave(events[last:], [])
    ag_end(0)
    events = ag_events(1)
    interleave(events[:-4], sequence_work(0))
    rs_start(0)
    interleave(events[-4:], [])
    ag_end(1)
    events = rs_events(0)
    interleave(events[:-4], [functools.partial(turned, 0)] + sequence_work(1))
    rs_start(1)
    interleave(events[-4:], [])
    rs_end(0)
    work = [functools.partial(turned, 1)] + [functools.partial(grad, j) for j in range(width // (2 * LANES))]
    work += [grads_start] + [functools.partial(give_back, 0, step) for step in range(groups)]
    interleave(rs_events(1), work)
    rs_end(1)
    for step in range(groups):
        give_back(1, step)
    for q in range(Q):
        tmine[0, q : q + 1, :] = uterms[:, q * piece : (q + 1) * piece]
    gain_start(0)
    grads_sum()
    gain_turn(0)
    took = taken(0)
    gain_end(0, ugrad_ref)
    took = took + taken(1)
    center = jnp.zeros((items, 1), F32)
    for q in range(Q):
        cols = slice(q * piece, (q + 1) * piece)
        h = hidden_ref[:, cols].astype(F32)
        d = took[q * items : (q + 1) * items]
        center += jnp.sum(igain_ref[:, cols] * d * h, axis=-1, keepdims=True)
        tmine[1, q : q + 1, :] = jnp.sum(d * h * ifactor, axis=0, keepdims=True)
    center = center / width
    gain_start(1)
    for q in range(Q):
        cols = slice(q * piece, (q + 1) * piece)
        h = hidden_ref[:, cols].astype(F32)
        d = took[q * items : (q + 1) * items]
        dhidden_ref[:, cols] = (
            ifactor * igain_ref[:, cols] * d - h * (ifactor * ifactor * ifactor * center)
        ).astype(BF16)
    gain_turn(1)
    for f in range(seqs):
        all_groups(out, arr, f, row_send, row_recv).wait_send()
        all_groups(back_out, back_arr, f, bk_send, bk_recv).wait_send()
        for d in range(2):
            for e in range(hops):
                ag_copy(f, d, e).wait_send()
                rs_copy(f, d, e).wait_send()
        for n in range(1 + 2 * hops):
            sb_copy(f, n).wait_send()
        for k in range(nz):
            mx_copy(f, k).wait_send()
    remote(grad_out.at[gsome], grad_out.at[gsome], gr_send, gr_recv, rep_peer(rep)).wait_send()
    remote(full_ref.at[gsome], full_ref.at[gsome], gg_send, gg_recv, rep_peer(rep)).wait()
    gain_end(1, igrad_ref)


def main(ng, ns, nd, cap, count, owner, row, hidden, igain, ugain, weight, dout):
    items, width = hidden.shape
    seqs, local_len = row.shape
    length = ns * local_len
    owners, msg = ns * nd, cap * Q
    piece = width // Q
    nr, nz = ng * nd, ns // 2
    hops = nz - 1
    cols = 3 * HD
    vmem = pl.BlockSpec(memory_space=pltpu.VMEM)
    full = (width // LANES, cols, LANES)
    dma = pltpu.SemaphoreType.DMA
    return pl.pallas_call(
        functools.partial(main_kernel, ng, ns, nd, cap),
        out_shape=(
            jax.ShapeDtypeStruct((seqs, length, HD), BF16),
            jax.ShapeDtypeStruct((items, width), BF16),
            jax.ShapeDtypeStruct(full, BF16),
            jax.ShapeDtypeStruct((1, width), F32),
            jax.ShapeDtypeStruct((1, width), F32),
        ),
        in_specs=[pl.BlockSpec(memory_space=pltpu.SMEM)] + [vmem] * 7,
        out_specs=[vmem] * 5,
        scratch_shapes=[
            pltpu.VMEM((owners, seqs, LANES), jnp.int32),
            pltpu.VMEM((owners, seqs, LANES), jnp.int32),
            pltpu.VMEM((seqs, owners * msg // LANES, 1, LANES), jnp.int32),
            pltpu.VMEM((Q * items, piece), BF16),
            pltpu.VMEM((seqs, owners, msg, piece), BF16),
            pltpu.VMEM((seqs, owners, msg, piece), BF16),
            pltpu.VMEM((seqs, Q * local_len, piece), BF16),
            pltpu.VMEM((seqs, owners, msg, piece), BF16),
            pltpu.VMEM((seqs, owners, msg, piece), BF16),
            pltpu.VMEM((seqs, local_len, width), BF16),
            pltpu.VMEM((seqs, local_len, 1), F32),
            pltpu.VMEM((seqs, local_len, width), BF16),
            pltpu.VMEM((1, width), F32),
            pltpu.VMEM((seqs, ns, local_len, width), BF16),
            pltpu.VMEM((seqs, length, cols), BF16),
            pltpu.VMEM((seqs, length, cols), BF16),
            pltpu.VMEM((cols, seqs * length), BF16),
            pltpu.VMEM((width, cols), BF16),
            pltpu.VMEM((seqs, ns, local_len, width), BF16),
            pltpu.VMEM((seqs, nz, local_len, width), BF16),
            pltpu.VMEM((seqs, 2, hops, local_len // 2, width), BF16),
            pltpu.VMEM((length, HD), F32),
            pltpu.VMEM((length, HD), F32),
            pltpu.VMEM(full, BF16),
            pltpu.VMEM((nr, full[0] // nr, cols, LANES), BF16),
            pltpu.VMEM((2, Q, piece), F32),
            pltpu.VMEM((2, ns, Q, piece), F32),
            pltpu.VMEM((2, nr, Q, piece), F32),
        ]
        + [dma] * 2
        + [dma((seqs,))] * 4
        + [dma((seqs, 2, hops))] * 2
        + [dma((seqs, 1 + 2 * hops))] * 2
        + [dma((seqs, nz))] * 2
        + [dma((seqs, 2, hops))] * 2
        + [dma] * 4
        + [dma((2,))] * 4,
        compiler_params=pltpu.CompilerParams(
            collective_id=0, has_side_effects=True, vmem_limit_bytes=VMEM_LIMIT
        ),
        name="main",
    )(count, owner, row, hidden, igain, ugain, weight, dout)


def finish_kernel(attn_in, dhidden_in, full_ref, ugrad_in, igrad_in, attn_ref, dhidden_ref, grad_ref, ugrad_ref, igrad_ref, sems):
    step = pl.program_id(0)

    def copies():
        pairs = ((attn_in, attn_ref), (dhidden_in, dhidden_ref), (ugrad_in, ugrad_ref), (igrad_in, igrad_ref))
        return [pltpu.make_async_copy(a, b, sems.at[n]) for n, (a, b) in enumerate(pairs)]

    @pl.when(step == 0)
    def _():
        for copy in copies():
            copy.start()

    for i in range(full_ref.shape[0]):
        grad_ref[0, i * LANES : (i + 1) * LANES, :] = full_ref[i].astype(F32).T

    @pl.when(step == pl.num_programs(0) - 1)
    def _():
        for copy in copies():
            copy.wait()


def finish(attn, dhidden, full, ugrad, igrad):
    chunks = full.shape[0]
    width = chunks * LANES
    anyspace = pl.BlockSpec(memory_space=pl.ANY)
    return pl.pallas_call(
        finish_kernel,
        grid=(3,),
        out_shape=(
            jax.ShapeDtypeStruct(attn.shape, BF16),
            jax.ShapeDtypeStruct(dhidden.shape, BF16),
            jax.ShapeDtypeStruct((3, width, HD), F32),
            jax.ShapeDtypeStruct(ugrad.shape, F32),
            jax.ShapeDtypeStruct(igrad.shape, F32),
        ),
        in_specs=[anyspace, anyspace, pl.BlockSpec((chunks, HD, LANES), lambda c: (0, c, 0)), anyspace, anyspace],
        out_specs=[anyspace, anyspace, pl.BlockSpec((1, width, HD), lambda c: (c, 0, 0)), anyspace, anyspace],
        scratch_shapes=[pltpu.SemaphoreType.DMA((4,))],
        name="finish",
    )(attn, dhidden, full, ugrad, igrad)


def local(
    item_hidden, item_gain, slot_owner, slot_row, seq_count, user_gain, query_key_value_weight, d_out
):
    ng, ns, nd = (lax.axis_size(a) for a in ("grp", "seq", "dp"))
    seqs, local_len, _ = slot_owner.shape
    width = item_hidden.shape[1]
    cap = max(2, 2 * local_len // (ns * nd))
    igain, ugain = item_gain.reshape(1, width), user_gain.reshape(1, width)
    owner = slot_owner.transpose(0, 2, 1)
    attn, d_hidden, full, ugrad, igrad = main(
        ng, ns, nd, cap, seq_count, owner, slot_row, item_hidden, igain, ugain, query_key_value_weight, d_out
    )
    attn, d_hidden, grads, ugrad, igrad = finish(attn, d_hidden, full, ugrad, igrad)
    return (attn, d_hidden, grads, ugrad.reshape(width), igrad.reshape(width))


def solution(mesh):
    in_specs = (
        P(("grp", "seq", "dp"), None),
        P(),
        P(("grp", "dp"), "seq", None),
        P(("grp", "dp"), "seq"),
        P(("grp", "dp")),
        P(),
        P(None, None, "seq"),
        P(("grp", "dp"), None, "seq"),
    )
    out_specs = (
        P(("grp", "dp"), None, "seq"),
        P(("grp", "seq", "dp"), None),
        P(None, None, "seq"),
        P(),
        P(),
    )
    return jax.shard_map(local, mesh=mesh, in_specs=in_specs, out_specs=out_specs, check_vma=False)
```

time: 253 us -> 254 us (level)
  the two profiles are of different devices: /device:TPU:88 before, /device:TPU:1 now
where the time goes in v2:
time: 254 us
  Pallas kernels  253 us (100%)
    pallas_call x1, Pallas kernels, main(): pl.pallas_call(functools.partial(main_kernel, ng, ns, nd, cap), out_shape...  217 us
    pallas_call x1, Pallas kernels, finish(): pl.pallas_call(finish_kernel, grid=(3,), out_shape=(jax.ShapeDtypeStruct(...  35.4 us

profile of v2, /device:TPU:1, one launch (start us, length us, event | category | flops | bytes accessed | tf_op | source)
XLA Modules:
  0.0 253.7 jit_solution(9996979987752104527)
XLA Ops:
  0.6 217.5 %main.1 = (bf16[2,1024,128]{2,1,0:T(8,128)(2,1)}, bf16[128,2048]{1,0:T(8,128)(2,1)}, bf16[16,384,128]{2,1,0:T(8,128)(2,1)}, f32[1,2048]{1,0:T(1,128)}, f32[1,2048]{1,0:T(1,128)}) custom-call(s32[2]{0:T(128)} %count_ref.1, s32[2,1,64]{2,1,0:T(1,128)} %bitcast.9, s32[2,64]{1,0:T(2,128)} %row_ref.1, bf16[128,2048]{1,0:T(8,128)(2,1)} %hidden_ref.1, ...), custom_call_target="tpu_custom_call" | custom-call | tf_op jit(solution)/shard_map/main/pallas_call | solution.py:543
  218.1 35.4 %finish.1 = (bf16[2,1024,128]{2,1,0:T(8,128)(2,1)}, bf16[128,2048]{1,0:T(8,128)(2,1)}, f32[3,2048,128]{2,1,0:T(8,128)}, f32[1,2048]{1,0:T(1,128)}, f32[1,2048]{1,0:T(1,128)}) custom-call(bf16[2,1024,128]{2,1,0:T(8,128)(2,1)} %get-tuple-element.15.attn_in, bf16[128,2048]{1,0:T(8,128)(2,1)} %get-tuple-element.16.dhidden_in, ...), custom_call_target="tpu_custom_call" | custom-call | tf_op jit(solution)/shard_map/finish/pallas_call | solution.py:624

commit v3 on v2

--- a/solution.py
+++ b/solution.py
@@ -57,15 +57,15 @@
 
 def main_kernel(
     ng, ns, nd, cap,
-    count_ref, owner_ref, row_ref, hidden_ref, igain_ref, ugain_ref, weight_ref, dout_ref,
+    count_ref, owner_ref, row_ref, hidden_ref, igain_ref, ugain_ref, weight_in, dout_in,
     attn_ref, dhidden_ref, full_ref, ugrad_ref, igrad_ref,
     req, reqr, val, table, out, arr, stack, back_out, back_arr,
     inputs, ufactor, dinputs, uterms,
     gat, prj, dpr, dpt, wgt, part, mix, ring, dk_acc, dv_acc,
-    grad_out, gin, tmine, tin, tmid,
+    grad_out, gin, tmine, tin, tmid, tall, picks, iterms, weight_ref, dout_ref, load_sem,
     id_send, id_recv, row_send, row_recv, bk_send, bk_recv,
     ag_send, ag_recv, sb_send, sb_recv, mx_send, mx_recv, rs_send, rs_recv,
-    gr_send, gr_recv, gg_send, gg_recv, t_send, t_recv, u_send, u_recv,
+    gr_send, gr_recv, gg_send, gg_recv, t_send, t_recv, u_send, u_recv, v_send, v_recv,
 ):
     seqs, _, local_len, width = gat.shape
     items = hidden_ref.shape[0]
@@ -96,10 +96,16 @@
         return {"grp": index // nd, "dp": lax.rem(index, nd)}
 
     def turn_of(step):
-        turn = (step + 1) // 2 if step % 2 else groups - step // 2
-        return lax.rem(my_group + turn, groups)
+        far = groups // 2 - (step + 1) // 2
+        return lax.rem(my_group + (far if step % 2 == 0 else groups - far), groups)
 
     barrier = pltpu.get_barrier_semaphore()
+    loads = (
+        pltpu.make_async_copy(weight_in, weight_ref, load_sem.at[0]),
+        pltpu.make_async_copy(dout_in, dout_ref, load_sem.at[1]),
+    )
+    for load in loads:
+        load.start()
 
     @pl.loop(1, owners)
     def _(i):
@@ -201,9 +207,10 @@
 
     def taken(f):
         back_arr[f, me] = back_out[f, me]
+        for g in range(groups):
+            picks[:, g * LANES : (g + 1) * LANES] = onehot(iota((Q * items, LANES), 0) == val[f, g].astype(F32))
         all_groups(back_out, back_arr, f, bk_send, bk_recv).wait_recv()
-        pick = jnp.concatenate([onehot(iota((Q * items, LANES), 0) == val[f, g].astype(F32)) for g in range(groups)], axis=1)
-        return jnp.dot(pick, back_arr[f].reshape(owners * msg, piece), preferred_element_type=F32)
+        return jnp.dot(picks[...], back_arr[f].reshape(owners * msg, piece), preferred_element_type=F32)
 
     def ag_place(f, d, e, origin):
         far = e // 2
@@ -322,14 +329,16 @@
                         got = got + ring[f, d, i].astype(F32)
             values = inputs[f, rows, :].astype(F32)
             factor = ufactor[f, rows, :]
-            term = jnp.sum(got * values * factor, axis=0, keepdims=True)
-            if f == 0 and h == 0:
-                uterms[...] = term
-            else:
-                uterms[...] += term
             weighted = ugain_ref[...] * got
             center = jnp.mean(weighted * values, axis=-1, keepdims=True)
-            dinputs[f, rows, :] = (factor * weighted - values * (factor * factor * factor * center)).astype(BF16)
+            d_in = factor * weighted - values * (factor * factor * factor * center)
+            dinputs[f, rows, :] = d_in.astype(BF16)
+            for ref, term in ((uterms, got * values * factor), (iterms, d_in * values)):
+                term = jnp.sum(term, axis=0, keepdims=True)
+                if f == 0 and h == 0:
+                    ref[...] = term
+                else:
+                    ref[...] += term
 
     def project(f, i):
         rows = gat[f, i * per : (i + 1) * per].reshape(tile, width)
@@ -393,10 +402,17 @@
     gmine = pl.ds(rep * gchunk, gchunk)
     gsome = pl.ds(0, (nr - 1) * gchunk)
 
+    away = sorted(
+        ((a, b) for a in range(ng) for b in range(nd) if a or b),
+        key=lambda o: (min(o[0], ng - o[0]) + min(o[1], nd - o[1]), (o[0] + 2 * o[1]) % 3, o),
+    )
+
+    def rep_at(a, b):
+        return lax.rem(grp + a, ng) * nd + lax.rem(dp + b, nd)
+
     def grads_start():
-        @pl.loop(1, nr)
-        def _(i):
-            peer = lax.rem(rep + i, nr)
+        for a, b in away:
+            peer = rep_at(a, b)
             remote(grad_out.at[pl.ds(peer * gchunk, gchunk)], gin.at[rep], gr_send, gr_recv, rep_peer(peer)).start()
 
         gin[rep] = grad_out[gmine]
@@ -408,38 +424,54 @@
             got += gin[i].astype(F32)
         full_ref[gmine] = got.astype(BF16)
 
-        @pl.loop(1, nr)
-        def _(i):
-            remote(full_ref.at[gmine], full_ref.at[gmine], gg_send, gg_recv, rep_peer(lax.rem(rep + i, nr))).start()
-
-    def gain_start(n):
-        tin[n, seq] = tmine[n]
+        for a, b in away:
+            remote(full_ref.at[gmine], full_ref.at[gmine], gg_send, gg_recv, rep_peer(rep_at(a, b))).start()
+
+    rp = 2 * Q // ns
+    tsome = pl.ds(0, ns - 1)
+
+    def gain_start():
+        for q in range(Q):
+            cols = slice(q * piece, (q + 1) * piece)
+            tmine[q] = iterms[:, cols] / igain_ref[:, cols]
+            tmine[Q + q] = uterms[:, cols]
 
         @pl.loop(1, ns)
         def _(i):
-            remote(tmine.at[n], tin.at[n, seq], t_send.at[n], t_recv.at[n], {"seq": lax.rem(seq + i, ns)}).start()
-
-    def gain_turn(n):
-        some = pl.ds(0, ns - 1)
-        remote(tin.at[n, some], tin.at[n, some], t_send.at[n], t_recv.at[n], {"seq": seq}).wait()
-        total = tin[n, 0]
+            peer = lax.rem(seq + i, ns)
+            remote(tmine.at[pl.ds(peer * rp, rp)], tin.at[seq], t_send, t_recv, {"seq": peer}).start()
+
+        tin[seq] = tmine[pl.ds(seq * rp, rp)]
+
+    def gain_turn():
+        remote(tin.at[tsome], tin.at[tsome], t_send, t_recv, {"seq": seq}).wait()
+        total = tin[0]
         for i in range(1, ns):
-            total = total + tin[n, i]
-        tmid[n, rep] = total
-
-        @pl.loop(1, nr)
+            total = total + tin[i]
+        tmid[rep] = total
+        for a, b in away:
+            remote(tmid.at[rep], tmid.at[rep], u_send, u_recv, rep_peer(rep_at(a, b))).start()
+
+    def gain_spread():
+        some = pl.ds(0, nr - 1)
+        remote(tmid.at[some], tmid.at[some], u_send, u_recv, rep_peer(rep)).wait()
+        total = tmid[0]
+        for i in range(1, nr):
+            total = total + tmid[i]
+        mine = pl.ds(seq * rp, rp)
+        tall[mine] = total
+
+        @pl.loop(1, ns)
         def _(i):
-            there = tmid.at[n, rep]
-            remote(there, there, u_send.at[n], u_recv.at[n], rep_peer(lax.rem(rep + i, nr))).start()
-
-    def gain_end(n, to_ref):
-        some = pl.ds(0, nr - 1)
-        remote(tmid.at[n, some], tmid.at[n, some], u_send.at[n], u_recv.at[n], rep_peer(rep)).wait()
-        total = tmid[n, 0]
-        for i in range(1, nr):
-            total = total + tmid[n, i]
+            remote(tall.at[mine], tall.at[mine], v_send, v_recv, {"seq": lax.rem(seq + i, ns)}).start()
+
+    def gain_end():
+        some = pl.ds(0, (ns - 1) * rp)
+        remote(tall.at[some], tall.at[some], v_send, v_recv, {"seq": seq}).wait()
         for q in range(Q):
-            to_ref[:, q * piece : (q + 1) * piece] = total[q : q + 1, :]
+            cols = slice(q * piece, (q + 1) * piece)
+            igrad_ref[:, cols] = tall[q]
+            ugrad_ref[:, cols] = tall[Q + q]
 
     def sequence_work(f):
         work = [functools.partial(project, f, i) for i in range(tiles)]
@@ -459,6 +491,8 @@
     for f in range(seqs):
         for step in range(groups):
             fetch(f, step)
+    for load in loads:
+        load.wait()
     for c in range(3):
         wgt[:, c * HD : (c + 1) * HD] = weight_ref[c]
     place(0)
@@ -479,31 +513,28 @@
     events = rs_events(0)
     interleave(events[:-4], [functools.partial(turned, 0)] + sequence_work(1))
     rs_start(1)
-    interleave(events[-4:], [])
+    work = [functools.partial(turned, 1)] + [functools.partial(grad, j) for j in range(width // (2 * LANES))]
+    interleave(events[-4:], work)
+    grads_start()
     rs_end(0)
-    work = [functools.partial(turned, 1)] + [functools.partial(grad, j) for j in range(width // (2 * LANES))]
-    work += [grads_start] + [functools.partial(give_back, 0, step) for step in range(groups)]
-    interleave(rs_events(1), work)
+    events = rs_events(1)
+    interleave(events[: len(events) // 2], [functools.partial(give_back, 0, step) for step in range(groups)])
+    interleave(events[len(events) // 2 :], [])
     rs_end(1)
+    gain_start()
     for step in range(groups):
         give_back(1, step)
-    for q in range(Q):
-        tmine[0, q : q + 1, :] = uterms[:, q * piece : (q + 1) * piece]
-    gain_start(0)
     grads_sum()
-    gain_turn(0)
+    gain_turn()
     took = taken(0)
-    gain_end(0, ugrad_ref)
+    gain_spread()
     took = took + taken(1)
     center = jnp.zeros((items, 1), F32)
     for q in range(Q):
         cols = slice(q * piece, (q + 1) * piece)
         h = hidden_ref[:, cols].astype(F32)
-        d = took[q * items : (q + 1) * items]
-        center += jnp.sum(igain_ref[:, cols] * d * h, axis=-1, keepdims=True)
-        tmine[1, q : q + 1, :] = jnp.sum(d * h * ifactor, axis=0, keepdims=True)
+        center += jnp.sum(igain_ref[:, cols] * took[q * items : (q + 1) * items] * h, axis=-1, keepdims=True)
     center = center / width
-    gain_start(1)
     for q in range(Q):
         cols = slice(q * piece, (q + 1) * piece)
         h = hidden_ref[:, cols].astype(F32)
@@ -511,7 +542,6 @@
         dhidden_ref[:, cols] = (
             ifactor * igain_ref[:, cols] * d - h * (ifactor * ifactor * ifactor * center)
         ).astype(BF16)
-    gain_turn(1)
     for f in range(seqs):
         all_groups(out, arr, f, row_send, row_recv).wait_send()
         all_groups(back_out, back_arr, f, bk_send, bk_recv).wait_send()
@@ -525,7 +555,7 @@
             mx_copy(f, k).wait_send()
     remote(grad_out.at[gsome], grad_out.at[gsome], gr_send, gr_recv, rep_peer(rep)).wait_send()
     remote(full_ref.at[gsome], full_ref.at[gsome], gg_send, gg_recv, rep_peer(rep)).wait()
-    gain_end(1, igrad_ref)
+    gain_end()
 
 
 def main(ng, ns, nd, cap, count, owner, row, hidden, igain, ugain, weight, dout):
@@ -549,7 +579,7 @@
             jax.ShapeDtypeStruct((1, width), F32),
             jax.ShapeDtypeStruct((1, width), F32),
         ),
-        in_specs=[pl.BlockSpec(memory_space=pltpu.SMEM)] + [vmem] * 7,
+        in_specs=[pl.BlockSpec(memory_space=pltpu.SMEM)] + [vmem] * 5 + [pl.BlockSpec(memory_space=pl.ANY)] * 2,
         out_specs=[vmem] * 5,
         scratch_shapes=[
             pltpu.VMEM((owners, seqs, LANES), jnp.int32),
@@ -577,9 +607,15 @@
             pltpu.VMEM((length, HD), F32),
             pltpu.VMEM(full, BF16),
             pltpu.VMEM((nr, full[0] // nr, cols, LANES), BF16),
-            pltpu.VMEM((2, Q, piece), F32),
-            pltpu.VMEM((2, ns, Q, piece), F32),
-            pltpu.VMEM((2, nr, Q, piece), F32),
+            pltpu.VMEM((2 * Q, 1, piece), F32),
+            pltpu.VMEM((ns, 2 * Q // ns, 1, piece), F32),
+            pltpu.VMEM((nr, 2 * Q // ns, 1, piece), F32),
+            pltpu.VMEM((2 * Q, 1, piece), F32),
+            pltpu.VMEM((Q * items, owners * msg), BF16),
+            pltpu.VMEM((1, width), F32),
+            pltpu.VMEM(weight.shape, BF16),
+            pltpu.VMEM(dout.shape, BF16),
+            dma((2,)),
         ]
         + [dma] * 2
         + [dma((seqs,))] * 4
@@ -588,7 +624,7 @@
         + [dma((seqs, nz))] * 2
         + [dma((seqs, 2, hops))] * 2
         + [dma] * 4
-        + [dma((2,))] * 4,
+        + [dma] * 6,
         compiler_params=pltpu.CompilerParams(
             collective_id=0, has_side_effects=True, vmem_limit_bytes=VMEM_LIMIT
         ),
@@ -596,31 +632,25 @@
     )(count, owner, row, hidden, igain, ugain, weight, dout)
 
 
-def finish_kernel(attn_in, dhidden_in, full_ref, ugrad_in, igrad_in, attn_ref, dhidden_ref, grad_ref, ugrad_ref, igrad_ref, sems):
-    step = pl.program_id(0)
-
-    def copies():
-        pairs = ((attn_in, attn_ref), (dhidden_in, dhidden_ref), (ugrad_in, ugrad_ref), (igrad_in, igrad_ref))
-        return [pltpu.make_async_copy(a, b, sems.at[n]) for n, (a, b) in enumerate(pairs)]
-
-    @pl.when(step == 0)
+def finish_kernel(attn_in, dhidden_in, full_ref, ugrad_in, igrad_in, attn_ref, dhidden_ref, grad_ref, ugrad_ref, igrad_ref):
+    @pl.when(pl.program_id(0) == 0)
     def _():
-        for copy in copies():
-            copy.start()
+        attn_ref[...] = attn_in[...]
+        dhidden_ref[...] = dhidden_in[...]
+        ugrad_ref[...] = ugrad_in[...]
+        igrad_ref[...] = igrad_in[...]
 
     for i in range(full_ref.shape[0]):
         grad_ref[0, i * LANES : (i + 1) * LANES, :] = full_ref[i].astype(F32).T
-
-    @pl.when(step == pl.num_programs(0) - 1)
-    def _():
-        for copy in copies():
-            copy.wait()
 
 
 def finish(attn, dhidden, full, ugrad, igrad):
     chunks = full.shape[0]
     width = chunks * LANES
-    anyspace = pl.BlockSpec(memory_space=pl.ANY)
+
+    def whole(a):
+        return pl.BlockSpec(a.shape, lambda c: (0,) * len(a.shape))
+
     return pl.pallas_call(
         finish_kernel,
         grid=(3,),
@@ -631,9 +661,8 @@
             jax.ShapeDtypeStruct(ugrad.shape, F32),
             jax.ShapeDtypeStruct(igrad.shape, F32),
         ),
-        in_specs=[anyspace, anyspace, pl.BlockSpec((chunks, HD, LANES), lambda c: (0, c, 0)), anyspace, anyspace],
-        out_specs=[anyspace, anyspace, pl.BlockSpec((1, width, HD), lambda c: (c, 0, 0)), anyspace, anyspace],
-        scratch_shapes=[pltpu.SemaphoreType.DMA((4,))],
+        in_specs=[whole(attn), whole(dhidden), pl.BlockSpec((chunks, HD, LANES), lambda c: (0, c, 0)), whole(ugrad), whole(igrad)],
+        out_specs=[whole(attn), whole(dhidden), pl.BlockSpec((1, width, HD), lambda c: (c, 0, 0)), whole(ugrad), whole(igrad)],
         name="finish",
     )(attn, dhidden, full, ugrad, igrad)
 

time: 254 us -> 195 us (0.77)
  Pallas kernels: 253 us -> 194 us
    pallas_call x1, Pallas kernels: 35.4 us -> 4.48 us  [finish(): pl.pallas_call(finish_kernel, grid=(3,), out_shape=(jax.ShapeDtypeStruct(...]
    pallas_call x1, Pallas kernels: 217 us -> 190 us  [main(): pl.pallas_call(functools.partial(main_kernel, ng, ns, nd, cap), out_shape...]
where the time goes in v3:
time: 195 us
  Pallas kernels  194 us (99%)
    pallas_call x1, Pallas kernels, main(): pl.pallas_call(functools.partial(main_kernel, ng, ns, nd, cap), out_shape...  190 us
    pallas_call x1, Pallas kernels, finish(): pl.pallas_call(finish_kernel, grid=(3,), out_shape=(jax.ShapeDtypeStruct(...  4.48 us

profile of v3, /device:TPU:1, one launch (start us, length us, event | category | flops | bytes accessed | tf_op | source)
XLA Modules:
  0.0 195.1 jit_solution(11811318734858527906)
XLA Ops:
  0.6 189.9 %main.1 = (bf16[2,1024,128]{2,1,0:T(8,128)(2,1)}, bf16[128,2048]{1,0:T(8,128)(2,1)}, bf16[16,384,128]{2,1,0:T(8,128)(2,1)}, f32[1,2048]{1,0:T(1,128)}, f32[1,2048]{1,0:T(1,128)}) custom-call(s32[2]{0:T(128)} %count_ref.1, s32[2,1,64]{2,1,0:T(1,128)} %bitcast.9, s32[2,64]{1,0:T(2,128)} %row_ref.1, bf16[128,2048]{1,0:T(8,128)(2,1)} %hidden_ref.1, ...), custom_call_target="tpu_custom_call" | custom-call | tf_op jit(solution)/shard_map/main/pallas_call | solution.py:573
  190.6 4.5 %finish.1 = (bf16[2,1024,128]{2,1,0:T(8,128)(2,1)}, bf16[128,2048]{1,0:T(8,128)(2,1)}, f32[3,2048,128]{2,1,0:T(8,128)}, f32[1,2048]{1,0:T(1,128)}, f32[1,2048]{1,0:T(1,128)}) custom-call(bf16[2,1024,128]{2,1,0:T(8,128)(2,1)} %get-tuple-element.15.attn_in, bf16[128,2048]{1,0:T(8,128)(2,1)} %get-tuple-element.16.dhidden_in, ...), custom_call_target="tpu_custom_call" | custom-call | tf_op jit(solution)/shard_map/finish/pallas_call | solution.py:654

commit v4 on v3

--- a/solution.py
+++ b/solution.py
@@ -182,11 +182,13 @@
         all_groups(out, arr, f, row_send, row_recv).wait_recv()
         arrived = arr[f].reshape(owners * msg, piece)
         total = jnp.zeros((local_len, 1), F32)
+        wanted_at = jnp.concatenate([base_col + q for q in range(Q)], axis=0)
+        put = jnp.concatenate(
+            [onehot(iota(wanted_at.shape, 1) + t * LANES == wanted_at) for t in range(groups)], axis=1
+        )
+        placed = jnp.dot(put, arrived, preferred_element_type=F32)
         for q in range(Q):
-            put = jnp.concatenate(
-                [onehot(iota((local_len, LANES), 1) + t * LANES == base_col + q) for t in range(groups)], axis=1
-            )
-            rows = jnp.dot(put, arrived, preferred_element_type=F32)
+            rows = placed[q * local_len : (q + 1) * local_len]
             inputs[f, :, q * piece : (q + 1) * piece] = rows.astype(BF16)
             total += jnp.sum(rows * rows, axis=-1, keepdims=True)
         factor = lax.rsqrt(total / width + EPS)
@@ -424,8 +426,46 @@
             got += gin[i].astype(F32)
         full_ref[gmine] = got.astype(BF16)
 
-        for a, b in away:
-            remote(full_ref.at[gmine], full_ref.at[gmine], gg_send, gg_recv, rep_peer(rep_at(a, b))).start()
+        for a in range(1, ng):
+            gg_own(0, {"grp": lax.rem(grp + a, ng)}).start()
+        for b in range(1, nd):
+            gg_own(1, {"dp": lax.rem(dp + b, nd)}).start()
+
+    def gg_own(way, device):
+        return remote(full_ref.at[gmine], full_ref.at[gmine], gg_send.at[way], gg_recv.at[way], device)
+
+    def gg_first(way):
+        some = full_ref.at[pl.ds(0, (ng if way == 0 else nd) * gchunk - gchunk)]
+        return remote(some, some, gg_send.at[way], gg_recv.at[way], rep_peer(rep))
+
+    def gg_half(way):
+        size = full_ref.shape[1] // 2
+        return pl.ds(way * size, size)
+
+    def gg_rest(way):
+        some = full_ref.at[pl.ds(0, (ng - 1) * (nd - 1) * gchunk), gg_half(way)]
+        return remote(some, some, gg_send.at[2 + way], gg_recv.at[2 + way], rep_peer(rep))
+
+    def grads_spread():
+        if ng > 1:
+            gg_first(0).wait_recv()
+        for a in range(1, ng):
+            there = full_ref.at[pl.ds(rep_at(a, 0) * gchunk, gchunk), gg_half(0)]
+            for b in range(1, nd):
+                remote(there, there, gg_send.at[2], gg_recv.at[2], {"dp": lax.rem(dp + b, nd)}).start()
+        if nd > 1:
+            gg_first(1).wait_recv()
+        for b in range(1, nd):
+            there = full_ref.at[pl.ds(rep_at(0, b) * gchunk, gchunk), gg_half(1)]
+            for a in range(1, ng):
+                remote(there, there, gg_send.at[3], gg_recv.at[3], {"grp": lax.rem(grp + a, ng)}).start()
+
+    def grads_end():
+        for way in range(2):
+            if (ng, nd)[way] > 1:
+                gg_first(way).wait_send()
+            if ng > 1 and nd > 1:
+                gg_rest(way).wait()
 
     rp = 2 * Q // ns
     tsome = pl.ds(0, ns - 1)
@@ -487,6 +527,8 @@
             for item in work[done:upto]:
                 item()
             done = upto
+        for item in work[done:]:
+            item()
 
     for f in range(seqs):
         for step in range(groups):
@@ -519,12 +561,14 @@
     rs_end(0)
     events = rs_events(1)
     interleave(events[: len(events) // 2], [functools.partial(give_back, 0, step) for step in range(groups)])
-    interleave(events[len(events) // 2 :], [])
+    interleave(events[len(events) // 2 : -2], [])
+    grads_sum()
+    interleave(events[-2:], [])
     rs_end(1)
     gain_start()
     for step in range(groups):
         give_back(1, step)
-    grads_sum()
+    grads_spread()
     gain_turn()
     took = taken(0)
     gain_spread()
@@ -554,7 +598,7 @@
         for k in range(nz):
             mx_copy(f, k).wait_send()
     remote(grad_out.at[gsome], grad_out.at[gsome], gr_send, gr_recv, rep_peer(rep)).wait_send()
-    remote(full_ref.at[gsome], full_ref.at[gsome], gg_send, gg_recv, rep_peer(rep)).wait()
+    grads_end()
     gain_end()
 
 
@@ -623,7 +667,8 @@
         + [dma((seqs, 1 + 2 * hops))] * 2
         + [dma((seqs, nz))] * 2
         + [dma((seqs, 2, hops))] * 2
-        + [dma] * 4
+        + [dma] * 2
+        + [dma((4,))] * 2
         + [dma] * 6,
         compiler_params=pltpu.CompilerParams(
             collective_id=0, has_side_effects=True, vmem_limit_bytes=VMEM_LIMIT

time: 195 us -> 185 us (0.949)
  Pallas kernels: 194 us -> 184 us
    pallas_call x1, Pallas kernels: 190 us -> 179 us  [main(): pl.pallas_call(functools.partial(main_kernel, ng, ns, nd, cap), out_shape...]
where the time goes in v4:
time: 185 us; the launch traced here: 184 us
  Pallas kernels  184 us (99%)
    pallas_call x1, Pallas kernels, main(): pl.pallas_call(functools.partial(main_kernel, ng, ns, nd, cap), out_shape...  179 us
    pallas_call x1, Pallas kernels, finish(): pl.pallas_call(finish_kernel, grid=(3,), out_shape=(jax.ShapeDtypeStruct(...  4.48 us

profile of v4, /device:TPU:1, one launch (start us, length us, event | category | flops | bytes accessed | tf_op | source)
XLA Modules:
  0.0 184.4 jit_solution(3856425942029344326)
XLA Ops:
  0.6 179.3 %main.1 = (bf16[2,1024,128]{2,1,0:T(8,128)(2,1)}, bf16[128,2048]{1,0:T(8,128)(2,1)}, bf16[16,384,128]{2,1,0:T(8,128)(2,1)}, f32[1,2048]{1,0:T(1,128)}, f32[1,2048]{1,0:T(1,128)}) custom-call(s32[2]{0:T(128)} %count_ref.1, s32[2,1,64]{2,1,0:T(1,128)} %bitcast.9, s32[2,64]{1,0:T(2,128)} %row_ref.1, bf16[128,2048]{1,0:T(8,128)(2,1)} %hidden_ref.1, ...), custom_call_target="tpu_custom_call" | custom-call | tf_op jit(solution)/shard_map/main/pallas_call | solution.py:617
  180.0 4.5 %finish.1 = (bf16[2,1024,128]{2,1,0:T(8,128)(2,1)}, bf16[128,2048]{1,0:T(8,128)(2,1)}, f32[3,2048,128]{2,1,0:T(8,128)}, f32[1,2048]{1,0:T(1,128)}, f32[1,2048]{1,0:T(1,128)}) custom-call(bf16[2,1024,128]{2,1,0:T(8,128)(2,1)} %get-tuple-element.15.attn_in, bf16[128,2048]{1,0:T(8,128)(2,1)} %get-tuple-element.16.dhidden_in, ...), custom_call_target="tpu_custom_call" | custom-call | tf_op jit(solution)/shard_map/finish/pallas_call | solution.py:699

commit v5 on v4

--- a/solution.py
+++ b/solution.py
@@ -561,9 +561,9 @@
     rs_end(0)
     events = rs_events(1)
     interleave(events[: len(events) // 2], [functools.partial(give_back, 0, step) for step in range(groups)])
-    interleave(events[len(events) // 2 : -2], [])
+    interleave(events[len(events) // 2 : -5], [])
     grads_sum()
-    interleave(events[-2:], [])
+    interleave(events[-5:], [])
     rs_end(1)
     gain_start()
     for step in range(groups):

time: 185 us -> 185 us (level)
  no operation moved by 1% of the time
where the time goes in v5:
time: 185 us; the launch traced here: 184 us
  Pallas kernels  184 us (99%)
    pallas_call x1, Pallas kernels, main(): pl.pallas_call(functools.partial(main_kernel, ng, ns, nd, cap), out_shape...  179 us
    pallas_call x1, Pallas kernels, finish(): pl.pallas_call(finish_kernel, grid=(3,), out_shape=(jax.ShapeDtypeStruct(...  4.48 us

profile of v5, /device:TPU:1, one launch (start us, length us, event | category | flops | bytes accessed | tf_op | source)
XLA Modules:
  0.0 184.4 jit_solution(14109550627917596465)
XLA Ops:
  0.6 179.3 %main.1 = (bf16[2,1024,128]{2,1,0:T(8,128)(2,1)}, bf16[128,2048]{1,0:T(8,128)(2,1)}, bf16[16,384,128]{2,1,0:T(8,128)(2,1)}, f32[1,2048]{1,0:T(1,128)}, f32[1,2048]{1,0:T(1,128)}) custom-call(s32[2]{0:T(128)} %count_ref.1, s32[2,1,64]{2,1,0:T(1,128)} %bitcast.9, s32[2,64]{1,0:T(2,128)} %row_ref.1, bf16[128,2048]{1,0:T(8,128)(2,1)} %hidden_ref.1, ...), custom_call_target="tpu_custom_call" | custom-call | tf_op jit(solution)/shard_map/main/pallas_call | solution.py:617
  180.0 4.5 %finish.1 = (bf16[2,1024,128]{2,1,0:T(8,128)(2,1)}, bf16[128,2048]{1,0:T(8,128)(2,1)}, f32[3,2048,128]{2,1,0:T(8,128)}, f32[1,2048]{1,0:T(1,128)}, f32[1,2048]{1,0:T(1,128)}) custom-call(bf16[2,1024,128]{2,1,0:T(8,128)(2,1)} %get-tuple-element.15.attn_in, bf16[128,2048]{1,0:T(8,128)(2,1)} %get-tuple-element.16.dhidden_in, ...), custom_call_target="tpu_custom_call" | custom-call | tf_op jit(solution)/shard_map/finish/pallas_call | solution.py:699
